TPU v7x, 256 devices: a whole 4x4x8 slice. The times are simulated.
256 devices in a mesh: row: 32 (over z, x), col: 8 (over y, core).
Axes of the slice: x: 4, y: 4, z: 8, core: 2. Of those that a mesh axis runs over, the one named last changes fastest.
Arguments:
- rhs: float32 [8, 32, 256, 128], P(None, 'row'), may hold values from -6 to 6
- inverse_low: bfloat16 [7, 32, 256, 2, 8, 256], P(None, 'row', None, None, 'col'), as said below
- inverse_top: bfloat16 [1, 32, 256, 4, 8, 256], P(None, 'row', None, None, 'col'), as said below
- lower_one: bfloat16 [2, 32, 256, 4, 8, 256], P(None, 'row', None, None, 'col')
- lower_two: bfloat16 [1, 32, 256, 12, 8, 256], P(None, 'row', None, None, 'col')
- lower_top: bfloat16 [1, 32, 256, 28, 8, 256], P(None, 'row', None, None, 'col'), as said below
- block_rows: int32 [256, 64], replicated, may hold values from -1 to 255, as said below
Outputs:
- solution: float32 [8, 32, 256, 128], P(None, 'row')
Inputs may be any that keep to these rules, and one draw needn't show every extreme that they name: `block_rows`: row j lists, in increasing order, distinct block rows of the separators that are ancestors of sep(j), then -1 to the end; the last block row 255 is listed by every block column below level 3. `inverse_low`: holds the full inverses of the separators' diagonal blocks. `inverse_top`: holds the full inverse of the top separator's diagonal block. `lower_top`: stored blocks that block_rows does not list hold values that are not entries of the factor.
All inputs are finite; a program needn't handle non-finite values.
Results may differ from a plain program's by a relative error of at most 0.0041.
Values may be sent and summed in bfloat16 or wider, within the bound.
No kernel may reach another device: no remote copies, remote signals or barrier semaphores. Data moves between devices by JAX's collectives and lax.ppermute only.
A program may use at most 64 MiB of HBM per device.

v0:
```python
import jax
import jax.numpy as jnp
from jax import lax
from jax.sharding import PartitionSpec as P

BLOCK = 256
SEP_BLOCKS = 16


def broadcast(value, axis, source):
    kept = jnp.where(lax.axis_index(axis) == source, value, 0).astype(value.dtype)
    return lax.psum(kept, axis)


def band_apply(tile, columns, position_of, keep):
    picked = jnp.take(columns, position_of, axis=0)
    if keep is not None:
        picked = jnp.where(keep[:, :, None, None], picked, jnp.zeros_like(picked))
    return jnp.einsum("lbkc,lkcr->lbr", tile, picked, preferred_element_type=jnp.float32)


def body(rhs, inverse_low, inverse_top, lower_one, lower_two, lower_top, block_rows):
    sep_count = SEP_BLOCKS
    row_index = lax.axis_index("row")
    col_index = lax.axis_index("col")
    n_rows = lax.axis_size("row")
    n_cols = lax.axis_size("col")
    group = n_rows // n_cols
    vector = rhs[:, 0]
    width = vector.shape[-1]
    diag_low = inverse_low[:, 0, :, :, 0, :]
    diag_top = inverse_top[:, 0, :, :, 0, :]
    band_one = lower_one[:, 0, :, :, 0, :]
    band_two = lower_two[:, 0, :, :, 0, :]
    band_top = lower_top[:, 0, :, :, 0, :]
    starts = [0, 8 * sep_count, 12 * sep_count, 14 * sep_count, 16 * sep_count]
    local = [value // n_rows for value in starts]

    def row_blocks(first, count):
        return first + jnp.arange(count, dtype=jnp.int32) * n_rows + row_index

    def col_offsets(first, count):
        return (first + jnp.arange(count, dtype=jnp.int32)) * n_cols + col_index

    def position(blocks, level):
        return (blocks // n_rows - local[level]) * group + blocks % n_rows // n_cols

    def listed(rows, cols):
        lists = jnp.take(block_rows, cols, axis=0)
        return jnp.any(lists == rows[:, None, None], axis=-1)

    def from_roots(piece):
        pieces = [broadcast(piece, "row", col_index + n_cols * step) for step in range(group)]
        return jnp.stack(pieces, axis=1).reshape(-1, BLOCK, width)

    def spread(piece):
        return from_roots(piece)

    def update(tile, rows, cols, sent_cols, level):
        return band_apply(tile, sent_cols, position(cols, level), listed(rows, cols))

    rows_one = row_blocks(starts[1], band_one.shape[0])
    rows_two = row_blocks(starts[2], band_two.shape[0])
    rows_top = row_blocks(starts[3], band_top.shape[0])
    child_one = 2 * (rows_one // sep_count - 8) * sep_count
    child_two = (8 + 2 * (rows_two // sep_count - 12)) * sep_count
    grand_two = 4 * (rows_two // sep_count - 12) * sep_count
    front_two = 4 * sep_count // n_cols
    partial_one = jnp.zeros((band_one.shape[0], BLOCK, width), jnp.float32)
    partial_two = jnp.zeros((band_two.shape[0], BLOCK, width), jnp.float32)
    partial_top = jnp.zeros((band_top.shape[0], BLOCK, width), jnp.float32)
    solved_parts = []
    for level in range(4):
        low, high = (local[level], local[level + 1])
        if level == 0:
            reduced = vector[low:high].astype(jnp.bfloat16)
        else:
            pending = (partial_one, partial_two, partial_top)[level - 1]
            lower_sum = lax.psum(pending, "col")
            reduced = (vector[low:high] - lower_sum).astype(jnp.bfloat16)
        reduced_cols = spread(reduced)
        if level < 3:
            tile = diag_low[low:high]
            rows_here = row_blocks(starts[level], high - low)
            targets = (rows_here // sep_count * sep_count)[:, None] + col_offsets(0, tile.shape[2])[
                None, :
            ]
        else:
            tile = diag_top
            targets = starts[3] + col_offsets(0, tile.shape[2])[None, :]
        diag_terms = band_apply(tile, reduced_cols, position(targets, level), None)
        solved = lax.psum(diag_terms, "col")
        solved_parts.append(solved)
        if level < 3:
            sent_cols = spread(solved.astype(jnp.bfloat16))
            top_first = starts[level] // n_cols
            top_count = (starts[level + 1] - starts[level]) // n_cols
            top_cols = col_offsets(top_first, top_count)[None, :]
            partial_top = partial_top + update(
                band_top[:, :, top_first : top_first + top_count],
                rows_top,
                top_cols,
                sent_cols,
                level,
            )
            if level == 0:
                one_cols = child_one[:, None] + col_offsets(0, band_one.shape[2])[None, :]
                partial_one = update(band_one, rows_one, one_cols, sent_cols, 0)
                two_cols = grand_two[:, None] + col_offsets(0, front_two)[None, :]
                partial_two = update(band_two[:, :, :front_two], rows_two, two_cols, sent_cols, 0)
            if level == 1:
                two_cols = (
                    child_two[:, None]
                    + col_offsets(front_two, band_two.shape[2] - front_two)[None, :]
                    - 4 * sep_count
                )
                partial_two = partial_two + update(
                    band_two[:, :, front_two:], rows_two, two_cols, sent_cols, 1
                )
    return jnp.concatenate(solved_parts, axis=0)[:, None]


def solution(mesh):
    return jax.shard_map(
        body,
        mesh=mesh,
        in_specs=(
            P(None, "row", None, None),
            P(None, "row", None, None, "col", None),
            P(None, "row", None, None, "col", None),
            P(None, "row", None, None, "col", None),
            P(None, "row", None, None, "col", None),
            P(None, "row", None, None, "col", None),
            P(),
        ),
        out_specs=P(None, "row", None, None),
        check_vma=False,
    )
```

profile of v0, /device:TPU:1, one launch (start us, length us, event | category | flops | bytes accessed | tf_op | source)
XLA Modules:
  0.0 1537.0 jit_solution(5537839340116053095)
XLA Ops:
  6.5 1.9 broadcast_select_fusion.3
  11.1 1.7 slice.55
  14.3 146.1 %all-reduce.48.cloned.1.call-done = (bf16[4,1,256,128]{3,2,1,0:T(8,128)(2,1)}, bf16[4,1,256,128]{3,2,1,0:T(8,128)(2,1)}, bf16[4,1,256,128]{3,2,1,0:T(8,128)(2,1)}, bf16[4,1,256,128]{3,2,1,0:T(8,128)(2,1)}) async-done(((bf16[4,1,256,128]{3,2,1,0:T(8,128)(2,1)}, bf16[4,1,256,128]{3,2,1,0:T(8,128)(2,1)}, bf16[4,1,256,128]{3,2,1,0:T(8,128)(2,1)}, bf16[4,1,256,128]{3,2,1,0:T(8,128)(2,1)}), ...) | async-done | bytes 1048592 | tf_op jit(solution)/shard_map/psum | solution.py:12
  162.6 2.5 convolution_bitcast_fusion
  165.2 65.7 %all-reduce.22.cloned.1.call-done = f32[4,256,128]{1,2,0:T(8,128)} async-done(((f32[4,256,128]{1,2,0:T(8,128)}), f32[4,256,128]{1,2,0:T(8,128)}) %all-reduce.22.cloned.1.call-update) | async-done | bytes 524304 | tf_op jit(solution)/shard_map/psum | solution.py:92
  230.9 1.8 select_bitcast_fusion.3
  235.8 145.9 %all-reduce.46.cloned.1.call-done = (bf16[4,1,256,128]{2,3,0,1:T(8,128)(2,1)}, bf16[4,1,256,128]{2,3,0,1:T(8,128)(2,1)}, bf16[4,1,256,128]{2,3,0,1:T(8,128)(2,1)}, bf16[4,1,256,128]{2,3,0,1:T(8,128)(2,1)}) async-done(((bf16[4,1,256,128]{2,3,0,1:T(8,128)(2,1)}, bf16[4,1,256,128]{2,3,0,1:T(8,128)(2,1)}, bf16[4,1,256,128]{2,3,0,1:T(8,128)(2,1)}, bf16[4,1,256,128]{2,3,0,1:T(8,128)(2,1)}), ...) | async-done | bytes 1048592 | tf_op jit(solution)/shard_map/psum | solution.py:12
  386.7 64.0 %all-reduce.24.cloned.1.call-done = f32[2,256,128]{1,2,0:T(8,128)} async-done(((f32[2,256,128]{1,2,0:T(8,128)}), f32[2,256,128]{1,2,0:T(8,128)}) %all-reduce.24.cloned.1.call-update) | async-done | bytes 262160 | tf_op jit(solution)/shard_map/psum | solution.py:79
  453.8 1.7 fusion.116
  455.4 143.4 %all-reduce.44.cloned.1.call-done = (bf16[2,1,256,128]{2,3,0,1:T(8,128)(2,1)}, bf16[2,1,256,128]{2,3,0,1:T(8,128)(2,1)}, bf16[2,1,256,128]{2,3,0,1:T(8,128)(2,1)}, bf16[2,1,256,128]{2,3,0,1:T(8,128)(2,1)}) async-done(((bf16[2,1,256,128]{2,3,0,1:T(8,128)(2,1)}, bf16[2,1,256,128]{2,3,0,1:T(8,128)(2,1)}, bf16[2,1,256,128]{2,3,0,1:T(8,128)(2,1)}, bf16[2,1,256,128]{2,3,0,1:T(8,128)(2,1)}), ...) | async-done | bytes 524304 | tf_op jit(solution)/shard_map/psum | solution.py:12
  608.5 60.2 %all-reduce.26.cloned.1.call-done = f32[2,256,128]{1,2,0:T(8,128)} async-done(((f32[2,256,128]{1,2,0:T(8,128)}), f32[2,256,128]{1,2,0:T(8,128)}) %all-reduce.26.cloned.1.call-update) | async-done | bytes 262160 | tf_op jit(solution)/shard_map/psum | solution.py:92
  677.4 139.6 %all-reduce.42.cloned.1.call-done = (bf16[2,1,256,128]{2,3,0,1:T(8,128)(2,1)}, bf16[2,1,256,128]{2,3,0,1:T(8,128)(2,1)}, bf16[2,1,256,128]{2,3,0,1:T(8,128)(2,1)}, bf16[2,1,256,128]{2,3,0,1:T(8,128)(2,1)}) async-done(((bf16[2,1,256,128]{2,3,0,1:T(8,128)(2,1)}, bf16[2,1,256,128]{2,3,0,1:T(8,128)(2,1)}, bf16[2,1,256,128]{2,3,0,1:T(8,128)(2,1)}, bf16[2,1,256,128]{2,3,0,1:T(8,128)(2,1)}), ...) | async-done | bytes 524304 | tf_op jit(solution)/shard_map/psum | solution.py:12
  820.6 2.7 fusion.6
  823.5 64.2 %all-reduce.28.cloned.1.call-done = f32[1,256,128]{1,2,0:T(8,128)} async-done(((f32[1,256,128]{1,2,0:T(8,128)}), f32[1,256,128]{1,2,0:T(8,128)}) %all-reduce.28.cloned.1.call-update) | async-done | bytes 131088 | tf_op jit(solution)/shard_map/psum | solution.py:79
  891.8 141.1 %all-reduce.40.cloned.1.call-done = (bf16[1,1,256,128]{2,3,1,0:T(8,128)(2,1)}, bf16[1,1,256,128]{2,3,1,0:T(8,128)(2,1)}, bf16[1,1,256,128]{2,3,1,0:T(8,128)(2,1)}, bf16[1,1,256,128]{2,3,1,0:T(8,128)(2,1)}) async-done(((bf16[1,1,256,128]{2,3,1,0:T(8,128)(2,1)}, bf16[1,1,256,128]{2,3,1,0:T(8,128)(2,1)}, bf16[1,1,256,128]{2,3,1,0:T(8,128)(2,1)}, bf16[1,1,256,128]{2,3,1,0:T(8,128)(2,1)}), ...) | async-done | bytes 262160 | tf_op jit(solution)/shard_map/psum | solution.py:12
  1035.4 63.9 %all-reduce.30.cloned.1.call-done = f32[1,256,128]{1,2,0:T(8,128)} async-done(((f32[1,256,128]{1,2,0:T(8,128)}), f32[1,256,128]{1,2,0:T(8,128)}) %all-reduce.30.cloned.1.call-update) | async-done | bytes 131088 | tf_op jit(solution)/shard_map/psum | solution.py:92
  1101.7 1.8 gather_fusion.8
  1104.1 2.6 convolution_bitcast_fusion.7
  1106.7 138.3 %all-reduce.38.cloned.1.call-done = (bf16[1,1,256,128]{2,3,1,0:T(8,128)(2,1)}, bf16[1,1,256,128]{2,3,1,0:T(8,128)(2,1)}, bf16[1,1,256,128]{2,3,1,0:T(8,128)(2,1)}, bf16[1,1,256,128]{2,3,1,0:T(8,128)(2,1)}) async-done(((bf16[1,1,256,128]{2,3,1,0:T(8,128)(2,1)}, bf16[1,1,256,128]{2,3,1,0:T(8,128)(2,1)}, bf16[1,1,256,128]{2,3,1,0:T(8,128)(2,1)}, bf16[1,1,256,128]{2,3,1,0:T(8,128)(2,1)}), ...) | async-done | bytes 262160 | tf_op jit(solution)/shard_map/psum | solution.py:12
  1248.0 3.4 fusion.4
  1251.5 63.9 %all-reduce.32.cloned.1.call-done = f32[1,256,128]{1,2,0:T(8,128)} async-done(((f32[1,256,128]{1,2,0:T(8,128)}), f32[1,256,128]{1,2,0:T(8,128)}) %all-reduce.32.cloned.1.call-update) | async-done | bytes 131088 | tf_op jit(solution)/shard_map/psum | solution.py:79
  1317.8 142.8 %all-reduce.36.cloned.1.call-done = (bf16[1,1,256,128]{2,3,1,0:T(8,128)(2,1)}, bf16[1,1,256,128]{2,3,1,0:T(8,128)(2,1)}, bf16[1,1,256,128]{2,3,1,0:T(8,128)(2,1)}, bf16[1,1,256,128]{2,3,1,0:T(8,128)(2,1)}) async-done(((bf16[1,1,256,128]{2,3,1,0:T(8,128)(2,1)}, bf16[1,1,256,128]{2,3,1,0:T(8,128)(2,1)}, bf16[1,1,256,128]{2,3,1,0:T(8,128)(2,1)}, bf16[1,1,256,128]{2,3,1,0:T(8,128)(2,1)}), ...) | async-done | bytes 262160 | tf_op jit(solution)/shard_map/psum | solution.py:12
  1462.1 2.0 convolution_bitcast_fusion.3
  1464.1 64.0 %all-reduce.34.cloned.1.call-done = f32[1,256,128]{1,2,0:T(8,128)} async-done(((f32[1,256,128]{1,2,0:T(8,128)}), f32[1,256,128]{1,2,0:T(8,128)}) %all-reduce.34.cloned.1.call-update) | async-done | bytes 131088 | tf_op jit(solution)/shard_map/psum | solution.py:92
  (166 shorter events, 58.1 us)
Async XLA Ops:
  6.5 378.1 %copy-start = (bf16[2,1,256,4,1,256]{5,3,4,2,1,0:T(4,128)(2,1)S(1)}, bf16[2,1,256,4,1,256]{5,3,4,2,1,0:T(4,128)(2,1)}, u32[]{:S(2)}) copy-start(bf16[2,1,256,4,1,256]{5,3,4,2,1,0:T(4,128)(2,1)} %param.16) | copy-start | bytes 3145732
  6.5 153.8 %all-reduce.48.cloned.1.call-start = ((), (), s32[]{:S(2)}) async-start(), calls=%async_computation.13 | async-start | bytes 2097152 | tf_op jit(solution)/shard_map/psum | solution.py:12
  9.4 221.5 %all-reduce.22.cloned.1.call-start = ((), (), s32[]{:S(2)}) async-start(), calls=%async_computation | async-start | bytes 1048576 | tf_op jit(solution)/shard_map/psum | solution.py:92
  165.1 216.7 %all-reduce.46.cloned.1.call-start = ((), (), s32[]{:S(2)}) async-start(), calls=%async_computation.12 | async-start | bytes 2097152 | tf_op jit(solution)/shard_map/psum | solution.py:12
  233.6 217.1 %all-reduce.24.cloned.1.call-start = ((), (), s32[]{:S(2)}) async-start(), calls=%async_computation.1 | async-start | bytes 524288 | tf_op jit(solution)/shard_map/psum | solution.py:79
  385.9 213.0 %all-reduce.44.cloned.1.call-start = ((), (), s32[]{:S(2)}) async-start(), calls=%async_computation.11 | async-start | bytes 1048576 | tf_op jit(solution)/shard_map/psum | solution.py:12
  453.1 149.7 %slice-start = ((bf16[7,1,256,2,1,256]{5,3,4,2,1,0:T(2,128)(2,1)}), bf16[2,1,256,2,1,256]{5,3,4,2,1,0:T(2,128)(2,1)S(1)}, s32[]{:S(2)}) async-start(bf16[7,1,256,2,1,256]{5,3,4,2,1,0:T(2,128)(2,1)} %param.14), calls=%async_computation.14 | async-start | bytes 1048576 | tf_op jit(solution)/shard_map/slice | solution.py:83
  453.1 215.6 %all-reduce.26.cloned.1.call-start = ((), (), s32[]{:S(2)}) async-start(), calls=%async_computation.2 | async-start | bytes 524288 | tf_op jit(solution)/shard_map/psum | solution.py:92
  603.9 213.2 %all-reduce.42.cloned.1.call-start = ((), (), s32[]{:S(2)}) async-start(), calls=%async_computation.10 | async-start | bytes 1048576 | tf_op jit(solution)/shard_map/psum | solution.py:12
  671.1 216.6 %all-reduce.28.cloned.1.call-start = ((), (), s32[]{:S(2)}) async-start(), calls=%async_computation.3 | async-start | bytes 262144 | tf_op jit(solution)/shard_map/psum | solution.py:79
  820.6 213.8 %slice-start.1 = ((bf16[7,1,256,2,1,256]{5,3,4,2,1,0:T(2,128)(2,1)}), bf16[1,1,256,2,1,256]{5,3,4,2,1,0:T(2,128)(2,1)S(1)}, s32[]{:S(2)}) async-start(bf16[7,1,256,2,1,256]{5,3,4,2,1,0:T(2,128)(2,1)} %param.14), calls=%async_computation.15 | async-start | bytes 524288 | tf_op jit(solution)/shard_map/slice | solution.py:83
  823.4 209.5 %all-reduce.40.cloned.1.call-start = ((), (), s32[]{:S(2)}) async-start(), calls=%async_computation.9 | async-start | bytes 524288 | tf_op jit(solution)/shard_map/psum | solution.py:12
  890.0 209.4 %all-reduce.30.cloned.1.call-start = ((), (), s32[]{:S(2)}) async-start(), calls=%async_computation.4 | async-start | bytes 262144 | tf_op jit(solution)/shard_map/psum | solution.py:92
  1035.4 209.7 %all-reduce.38.cloned.1.call-start = ((), (), s32[]{:S(2)}) async-start(), calls=%async_computation.8 | async-start | bytes 524288 | tf_op jit(solution)/shard_map/psum | solution.py:12
  1101.6 213.8 %all-reduce.32.cloned.1.call-start = ((), (), s32[]{:S(2)}) async-start(), calls=%async_computation.5 | async-start | bytes 262144 | tf_op jit(solution)/shard_map/psum | solution.py:79
  1104.1 142.5 %copy-start.8 = (pred[4]{0:T(512)(128)(4,1)S(1)}, pred[4]{0:T(512)(128)(4,1)}, u32[]{:S(2)}) copy-start(pred[4]{0:T(512)(128)(4,1)} %fusion.83) | copy-start | bytes 16
  1104.1 143.8 %copy-start.3 = (bf16[16,256,128]{2,1,0:T(8,128)(2,1)S(1)}, bf16[16,256,128]{2,1,0:T(8,128)(2,1)}, u32[]{:S(2)}) copy-start(bf16[16,256,128]{2,1,0:T(8,128)(2,1)} %gather_fusion.8) | copy-start | bytes 3145732
  1104.1 143.8 %copy-start.9 = (pred[16]{0:T(512)(128)(4,1)S(1)}, pred[16]{0:T(512)(128)(4,1)}, u32[]{:S(2)}) copy-start(pred[16]{0:T(512)(128)(4,1)} %get-tuple-element.79) | copy-start | bytes 52
  1106.7 141.2 %copy-start.10 = (f32[128,256]{1,0:T(8,128)S(1)}, f32[128,256]{1,0:T(8,128)}, u32[]{:S(2)}) copy-start(f32[128,256]{1,0:T(8,128)} %convolution_bitcast_fusion.7) | copy-start | bytes 393220
  1251.3 276.8 %copy-start.1 = (f32[4,256,128]{1,2,0:T(8,128)S(1)}, f32[4,256,128]{1,2,0:T(8,128)}, u32[]{:S(2)}) copy-start(f32[4,256,128]{1,2,0:T(8,128)} %all-reduce.22.cloned.1.call-done) | copy-start | bytes 1572868
  1251.3 276.8 %copy-start.4 = (f32[2,256,128]{1,2,0:T(8,128)S(1)}, f32[2,256,128]{1,2,0:T(8,128)}, u32[]{:S(2)}) copy-start(f32[2,256,128]{1,2,0:T(8,128)} %all-reduce.26.cloned.1.call-done) | copy-start | bytes 786436
  1251.3 276.8 %copy-start.5 = (f32[1,256,128]{1,2,0:T(8,128)S(1)}, f32[1,256,128]{1,2,0:T(8,128)}, u32[]{:S(2)}) copy-start(f32[1,256,128]{1,2,0:T(8,128)} %all-reduce.30.cloned.1.call-done) | copy-start | bytes 393220
  1251.4 209.2 %all-reduce.36.cloned.1.call-start = ((), (), s32[]{:S(2)}) async-start(), calls=%async_computation.7 | async-start | bytes 524288 | tf_op jit(solution)/shard_map/psum | solution.py:12
  1317.6 210.5 %all-reduce.34.cloned.1.call-start = ((), (), s32[]{:S(2)}) async-start(), calls=%async_computation.6 | async-start | bytes 262144 | tf_op jit(solution)/shard_map/psum | solution.py:92
  (4 other events, 145.4 us)
Sparse Core Ops, SparseCore 0:
  11.2 149.1 all-reduce.47
  165.2 65.5 all-reduce.21
  235.2 146.5 all-reduce.45
  386.0 64.6 all-reduce.23
  454.3 144.4 all-reduce.43
  604.0 64.6 all-reduce.25
  672.5 144.4 all-reduce.41
  823.5 64.1 all-reduce.27
  891.6 141.2 all-reduce.39
  1035.5 63.8 all-reduce.29
  1103.7 141.2 all-reduce.37
  1251.5 63.8 all-reduce.31
  1319.3 141.2 all-reduce.35
  1464.3 63.8 all-reduce.33
where the time goes:
time: 1540 us
  waiting for transfers between devices  1440 us (94%)
  other arithmetic  38.4 us (2%)
  local copies, waits for them, and re-layouts  21.9 us (1%)
  matrix products  19.1 us (1%)
    psum x7, waiting for transfers between devices, broadcast(): return lax.psum(kept, axis)  997 us
    psum x4, waiting for transfers between devices, body(): solved = lax.psum(diag_terms, 'col')  254 us
    psum x3, waiting for transfers between devices, body(): lower_sum = lax.psum(pending, 'col')  192 us
  transfers between devices with their start and end apart: 14, of which 14 were waited for; matrix products, arithmetic and copies ran while one was open for 2% of the time, Pallas kernels for 0%

commit v1 on v0

v1 whole, which is shorter than its diff:
```python
import jax
import jax.numpy as jnp
from jax import lax
from jax.experimental import pallas as pl
from jax.experimental.pallas import tpu as pltpu
from jax.sharding import PartitionSpec as P

AXES = ("row", "col")
BF = jnp.bfloat16
F32 = jnp.float32
N = 256


def ring(a, b, n):
    d = (a - b) % n
    return min(d, n - d)


def row_hops(a, b):
    return ring(a // 4, b // 4, 8) + ring(a % 4, b % 4, 4)


def col_hops(a, b):
    return 2 * ring(a // 2, b // 2, 4) + (a % 2 != b % 2)


def spread_pairs(shift):
    pairs = []
    for m in range(4):
        for q in range(8):
            source = 8 * (m ^ shift) + q
            rows = sorted(range(8 * m, 8 * m + 8), key=lambda o: -row_hops(o, source))
            cols = sorted(range(8), key=lambda t: col_hops(t, q))
            pairs += [(source * 8 + t, o * 8 + q) for o, t in zip(rows, cols)]
    return sorted(pairs)


def turn_table():
    table = []
    for r in range(8):
        rows = sorted(range(8), key=lambda o: -row_hops(o, r))
        cols = sorted(range(8), key=lambda t: col_hops(t, r))
        line = [0] * 8
        for o, t in zip(rows, cols):
            line[t] = o
        table.append(line)
    return table


def turn_pairs():
    table = turn_table()
    return [
        ((8 * m + r) * 8 + t, (8 * m + table[r][t]) * 8 + r)
        for m in range(4)
        for r in range(8)
        for t in range(8)
    ]


def send(value, pairs):
    return lax.ppermute(value, AXES, pairs)


def dot(tile, block):
    return lax.dot_general(tile, block, (((1,), (1,)), ((), ())), preferred_element_type=F32)


def at(array, index, axis=0):
    return lax.dynamic_index_in_dim(array, index, axis, keepdims=False)


def params():
    return pltpu.CompilerParams(vmem_limit_bytes=24 * 1024 * 1024)


def whole(*_):
    return pl.BlockSpec(memory_space=pltpu.VMEM)


def diagonal0(place, near, far, tiles):
    def kernel(s, near_ref, far_ref, tile_ref, out_ref):
        e = s[1]
        for a in range(4):
            value = dot(tile_ref[a, e], near_ref[a]) + dot(tile_ref[a, 1 - e], far_ref[a])
            out_ref[:, a] = value.T.reshape(8, 16, 256).astype(BF)

    return pl.pallas_call(
        kernel,
        out_shape=jax.ShapeDtypeStruct((8, 4, 16, 256), BF),
        in_specs=[pl.BlockSpec(memory_space=pltpu.SMEM), whole(), whole(), whole()],
        out_specs=whole(),
        compiler_params=params(),
        name="diagonal0",
    )(place, near, far, tiles)


def lower0(place, keep, slices, one, two, last):
    def kernel(s, k, x_ref, one_ref, two_ref, last_ref, out_ref, acc):
        c, h = pl.program_id(0), s[3]

        def term(pairs):
            tiles = jnp.concatenate([tile for _, tile, _ in pairs], axis=1)
            blocks = []
            for a0, _, flag in pairs:
                block = jnp.concatenate([x_ref[p, a0] for p in range(8)], axis=0)
                blocks.append(jnp.where(flag != 0, block, jnp.zeros_like(block)))
            return dot(tiles, jnp.concatenate(blocks, axis=1))

        sums = [
            term([(h, one_ref[0, 0], k[4 * h + c])]),
            term([(2 + h, one_ref[1, 0], k[32 + 8 + 4 * h + c])]),
            term([(2 * h + b, two_ref[b, 0], k[64 + 8 * h + 4 * b + c]) for b in range(2)]),
            term([(a0, last_ref[a0, 0], k[96 + 4 * a0 + c]) for a0 in range(4)]),
        ]

        @pl.when(c == 0)
        def _():
            for i in range(4):
                acc[i] = sums[i]

        @pl.when(c != 0)
        def _():
            for i in range(4):
                acc[i] += sums[i]

        @pl.when(c == 3)
        def _():
            for i in range(4):
                value = acc[i].T.astype(BF)
                for p in range(8):
                    out_ref[s[4 + p], i] = value[16 * p : 16 * p + 16]

    return pl.pallas_call(
        kernel,
        out_shape=jax.ShapeDtypeStruct((8, 4, 16, 256), BF),
        grid_spec=pltpu.PrefetchScalarGridSpec(
            num_scalar_prefetch=2,
            grid=(4,),
            in_specs=[
                pl.BlockSpec((8, 4, 16, 256), lambda c, s, k: (c, 0, 0, 0)),
                pl.BlockSpec((2, 1, 256, 256), lambda c, s, k: (0, c, 0, 0)),
                pl.BlockSpec((2, 1, 256, 256), lambda c, s, k: (0, c, 0, 0)),
                pl.BlockSpec((4, 1, 256, 256), lambda c, s, k: (0, c, 0, 0)),
            ],
            out_specs=pl.BlockSpec((8, 4, 16, 256), lambda c, s, k: (0, 0, 0, 0)),
            scratch_shapes=[pltpu.VMEM((4, 256, 128), F32)],
        ),
        compiler_params=params(),
        name="lower0",
    )(place, keep, slices, one, two, last)


def multiply(place, terms, base, n_out, copies, dtype, name, token=None):
    steps = terms[0][3]

    def kernel(s, *refs):
        step = pl.program_id(0)
        copy_ref, out_ref, acc = refs[-3:]
        h = s[3]
        tiles, blocks = [[] for _ in range(n_out)], [[] for _ in range(n_out)]
        for n, (_, _, _, _, _, picks) in enumerate(terms):
            x_ref, tile_ref = refs[2 * n : 2 * n + 2]
            for t, c, a, o in picks(step, h):
                for j in range(8):
                    tiles[o].append(tile_ref[j, t])
                    blocks[o].append(x_ref[8 * c + j, a])
        for o in range(n_out):
            value = dot(jnp.concatenate(tiles[o], axis=1), jnp.concatenate(blocks[o], axis=1))

            @pl.when(step == 0)
            def _():
                acc[o] = value

            @pl.when(step != 0)
            def _():
                acc[o] += value

        @pl.when(step == steps - 1)
        def _():
            for o in range(n_out):
                value = acc[o].T
                if base is not None:
                    value = refs[2 * len(terms)][o] - value
                out_ref[o] = value
                cast = value.astype(dtype)
                for r in range(copies):
                    copy_ref[r, o] = cast

    args, specs, size = [], [], 0
    for x, tiles, first, _, count, _ in terms:
        args += [x, tiles]
        specs.append(pl.BlockSpec(x.shape, lambda i, s: (0, 0, 0, 0)))
        specs.append(
            pl.BlockSpec((8, count, 256, 256), lambda i, s, f=first // count: (0, f + i, 0, 0))
        )
        size += 8 * count * steps * 256 * 256
    if base is not None:
        args.append(base)
        specs.append(pl.BlockSpec(base.shape, lambda i, s: (0, 0, 0)))
    if token is not None:
        args.append(token)
        specs.append(pl.BlockSpec(token.shape, lambda i, s: (0, 0)))
    return pl.pallas_call(
        kernel,
        out_shape=(
            jax.ShapeDtypeStruct((copies, n_out, 16, 256), dtype),
            jax.ShapeDtypeStruct((n_out, 16, 256), F32),
        ),
        grid_spec=pltpu.PrefetchScalarGridSpec(
            num_scalar_prefetch=1,
            grid=(steps,),
            in_specs=specs,
            out_specs=(
                pl.BlockSpec((copies, n_out, 16, 256), lambda i, s: (0, 0, 0, 0)),
                pl.BlockSpec((n_out, 16, 256), lambda i, s: (0, 0, 0)),
            ),
            scratch_shapes=[pltpu.VMEM((n_out, 256, 16), F32)],
        ),
        compiler_params=params(),
        cost_estimate=pl.CostEstimate(flops=256 * size, bytes_accessed=2 * size, transcendentals=0),
        name=name,
    )(place, *args)


def assemble_early(slices):
    def kernel(x_ref, out_ref):
        out_ref[0] = x_ref[:, 0].reshape(128, 256).T

    return pl.pallas_call(
        kernel,
        out_shape=jax.ShapeDtypeStruct((8, 256, 128), F32),
        grid=(6,),
        in_specs=[pl.BlockSpec((8, 1, 16, 256), lambda i: (0, i, 0, 0))],
        out_specs=pl.BlockSpec((1, 256, 128), lambda i: (i, 0, 0)),
        compiler_params=params(),
        name="assemble_early",
    )(slices)


def assemble_late(early, slices):
    def kernel(x_ref, _, out_ref):
        out_ref[0] = x_ref[:, 0].reshape(128, 256).T

    return pl.pallas_call(
        kernel,
        out_shape=jax.ShapeDtypeStruct((8, 256, 128), F32),
        grid=(2,),
        in_specs=[
            pl.BlockSpec((8, 1, 16, 256), lambda i: (0, i, 0, 0)),
            pl.BlockSpec(memory_space=pl.ANY),
        ],
        out_specs=pl.BlockSpec((1, 256, 128), lambda i: (6 + i, 0, 0)),
        input_output_aliases={1: 0},
        compiler_params=params(),
        name="assemble_late",
    )(slices, early)


HALVES = [list(range(16)), list(range(16, 32))]


def exchange(copies, axis, groups=None):
    return lax.all_to_all(copies, axis, 0, 0, tiled=True, axis_index_groups=groups)


def swap(value, mask):
    return send(value, [(i, i ^ mask) for i in range(256)])


def finish0(sums, upper, token):
    def kernel(x_ref, upper_ref, _, copy_ref, two_ref, three_ref):
        value = upper_ref[...] - jnp.sum(x_ref[...].astype(F32), axis=0)
        two_ref[...] = value[2:3]
        three_ref[...] = value[3:4]
        cast = value[0:2].astype(BF)
        for r in range(16):
            copy_ref[r] = cast

    slot = jax.ShapeDtypeStruct((1, 16, 256), F32)
    return pl.pallas_call(
        kernel,
        out_shape=(jax.ShapeDtypeStruct((16, 2, 16, 256), BF), slot, slot),
        compiler_params=params(),
        name="finish0",
    )(sums, upper, token)


def arrived(tiles):
    return tiles[0, 0, 0:16, 0:128]


def body(rhs, inverse_low, inverse_top, lower_one, lower_two, lower_top, block_rows):
    row = lax.axis_index("row")
    col = lax.axis_index("col")
    m, h, e, core = row // 8, row // 16, row // 8 % 2, col % 2
    table = turn_table()
    owner = [[line.index(p) for p in range(8)] for line in table]
    place = jnp.concatenate(
        [jnp.stack([m, e, core, h]), at(jnp.array(owner, jnp.int32), col), col[None]]
    ).astype(jnp.int32)
    sent0 = jnp.swapaxes(rhs[0:4, 0], 1, 2).astype(BF)
    near = send(sent0, spread_pairs(0))
    far = send(sent0, spread_pairs(1))

    lists = at(block_rows.reshape(32, 8, 64), col, 1)
    targets = jnp.stack([128 + row, 160 + row, 192 + row, 224 + row])
    listed = jnp.any(lists[None] == targets[:, None, None], axis=-1)
    keep = listed.astype(jnp.int32).reshape(128)

    def masked(tiles, flags):
        return jnp.where(flags[:, None, None], tiles, jnp.zeros_like(tiles))

    two = jnp.swapaxes(lower_two[0, 0, :, :, 0, :], 0, 1).reshape(3, 4, 256, 256)
    last = jnp.swapaxes(lower_top[0, 0, :, :, 0, :], 0, 1).reshape(7, 4, 256, 256)
    first = jnp.concatenate(
        [
            jnp.swapaxes(inverse_low[4:6, 0, :, :, 0, :], 1, 2).reshape(4, 256, 256),
            masked(two[2], lax.dynamic_slice(listed[2], (16 + 4 * h,), (4,))),
            jnp.swapaxes(inverse_low[6, 0, :, :, 0, :], 0, 1),
        ]
    )
    gate = near[0, 0, 0] * 0
    first = lax.all_gather(first + gate, "col")
    low, one, upper = lax.optimization_barrier((inverse_low[0:4], lower_one, rhs[4:8, 0]))
    low = jnp.swapaxes(low[:, 0, :, :, 0, :], 1, 2)
    one = jnp.swapaxes(one[:, 0, :, :, 0, :], 1, 2)
    upper = lax.dynamic_slice(jnp.swapaxes(upper, 1, 2), (0, 16 * col, 0), (4, 16, 256))
    near, far, last_later, inverse_top = lax.optimization_barrier((near, far, last[4:7], inverse_top))
    second = lax.all_gather(masked(last_later.reshape(12, 256, 256), listed[3, 16:28]) + gate, "col")
    third = lax.all_gather(jnp.swapaxes(inverse_top[0, 0, :, :, 0, :], 0, 1) + gate, "col")

    near, far, keep, upper, one = lax.optimization_barrier((near, far, keep, upper, one))

    sums = exchange(diagonal0(place, near, far, low), "col")
    solved0 = jnp.sum(sums.astype(F32), axis=0)
    slices = send(solved0.astype(BF), turn_pairs())
    slices, one = lax.optimization_barrier((slices, one))
    slices = exchange(jnp.broadcast_to(slices, (32, 4, 16, 256)), "row")
    sums = exchange(lower0(place, keep, slices, one, two, last), "col")
    copies, base2, base3 = finish0(sums, upper, arrived(first))

    reduced = exchange(copies, "row", HALVES)
    copies, solved1 = multiply(
        place, [(reduced, first, 0, 1, 4, lambda i, h: [(t, t % 2, t // 2, t // 2) for t in range(4)])], None, 2, 32, BF, "diagonal1"
    )
    x1 = exchange(copies, "row")
    early = lax.all_gather(jnp.concatenate([solved0, solved1, solved1]), "col")

    copies, _ = multiply(
        place, [(x1, first, 4, 4, 1, lambda i, h: [(0, i, h, 0)])], base2, 1, 16, BF, "lower2"
    )
    reduced = exchange(copies, "row", HALVES)
    copies, solved2 = multiply(
        place, [(reduced, first, 8, 2, 1, lambda i, h: [(0, i, 0, 0)])], None, 1, 32, BF, "diagonal2", arrived(second)
    )
    x2 = exchange(copies, "row")

    copies, _ = multiply(
        place,
        [
            (x1, second, 0, 4, 2, lambda i, h: [(t, (2 * i + t) % 4, i // 2, 0) for t in range(2)]),
            (x2, second, 8, 4, 1, lambda i, h: [(0, i, 0, 0)]),
        ],
        base3, 1, 32, BF, "lower3", arrived(third),
    )
    reduced = exchange(copies, "row")
    _, solved3 = multiply(
        place, [(reduced, third, 0, 4, 1, lambda i, h: [(0, i, 0, 0)])], None, 1, 1, BF, "diagonal3"
    )
    late = jnp.concatenate([solved2, solved3])
    late = exchange(jnp.broadcast_to(late, (8, 2, 16, 256)), "col")
    return assemble_late(assemble_early(early), late)[:, None]


def solution(mesh):
    return jax.shard_map(
        body,
        mesh=mesh,
        in_specs=(
            P(None, "row", None, None),
            P(None, "row", None, None, "col", None),
            P(None, "row", None, None, "col", None),
            P(None, "row", None, None, "col", None),
            P(None, "row", None, None, "col", None),
            P(None, "row", None, None, "col", None),
            P(),
        ),
        out_specs=P(None, "row", None, None),
        check_vma=False,
    )
```

time: 1540 us -> 259 us (0.17)
  waiting for transfers between devices: 1440 us -> 47.9 us
  blocking collectives: 0 us -> 87.9 us
  starting transfers between devices: 0.55 us -> 43.2 us
  other arithmetic: 38.4 us -> 5.69 us
  Pallas kernels: 0 us -> 25.6 us
  matrix products: 19.1 us -> 0 us
    psum x14 -> x0, waiting for transfers between devices: 1440 us -> none  [the longest x7 997 us: broadcast(): return lax.psum(kept, axis)]
    all_to_all x0 -> x4, blocking collectives: none -> 87.9 us  [exchange(): lax.all_to_all(copies, axis, 0, 0, tiled=True, axis_index_groups=groups)]
    all_to_all x0 -> x5, waiting for transfers between devices: none -> 36.2 us  [exchange(): lax.all_to_all(copies, axis, 0, 0, tiled=True, axis_index_groups=groups)]
    all_to_all x0 -> x5, starting transfers between devices: none -> 30.7 us  [exchange(): lax.all_to_all(copies, axis, 0, 0, tiled=True, axis_index_groups=groups)]
    pallas_call x0 -> x10, Pallas kernels: none -> 25.6 us  [the longest x5 17.5 us: multiply(): pl.pallas_call(kernel, out_shape=(jax.ShapeDtypeStruct((copies, n_out, 16...]
    unnamed x26 -> x22, local copies, waits for them, and re-layouts: 1.36 us -> 21.3 us
    another operation x16 -> x1, other arithmetic: 19.2 us -> 0.08 us  [body(): targets = jnp.stack([128 + row, 160 + row, 192 + row, 224 + row])]
    dot_general x10 -> x0, matrix products: 19.1 us -> none  [band_apply(): jnp.einsum('lbkc,lkcr->lbr', tile, picked, preferred_element_type=jnp.flo...]
  transfers between devices with their start and end apart: 14 -> 12, of which waited for: 14 -> 8; matrix products, arithmetic and copies ran while one was open for 2% -> 6% of each run, Pallas kernels for 0% -> 10%
where the time goes in v1:
time: 259 us; the launch traced here: 258 us
  blocking collectives  87.9 us (34%)
  waiting for transfers between devices  47.9 us (18%)
  starting transfers between devices  43.2 us (17%)
  local copies, waits for them, and re-layouts  33.3 us (13%)
  Pallas kernels  25.6 us (10%)
  between operations  14.1 us (5%)
  other arithmetic  5.69 us (2%)
    all_to_all x4, blocking collectives, exchange(): lax.all_to_all(copies, axis, 0, 0, tiled=True, axis_index_groups=groups)  87.9 us
    all_to_all x5, waiting for transfers between devices, exchange(): lax.all_to_all(copies, axis, 0, 0, tiled=True, axis_index_groups=groups)  36.2 us
    all_to_all x5, starting transfers between devices, exchange(): lax.all_to_all(copies, axis, 0, 0, tiled=True, axis_index_groups=groups)  30.7 us
    unnamed x22, local copies, waits for them, and re-layouts  21.3 us
    pallas_call x5, Pallas kernels, multiply(): pl.pallas_call(kernel, out_shape=(jax.ShapeDtypeStruct((copies, n_out, 16...  17.5 us
    ppermute x3, starting transfers between devices, send(): return lax.ppermute(value, AXES, pairs)  12.3 us
    all_gather x1, waiting for transfers between devices, body(): lax.all_gather(jnp.swapaxes(inverse_top[0, 0, :, :, 0, :], 0, 1) + gate,...  6.53 us
  transfers between devices with their start and end apart: 12, of which 8 were waited for; matrix products, arithmetic and copies ran while one was open for 6% of the time, Pallas kernels for 10%

profile of v1, /device:TPU:1, one launch (start us, length us, event | category | flops | bytes accessed | tf_op | source)
XLA Modules:
  0.0 257.6 jit_solution(1018663435365088032)
XLA Ops:
  7.8 4.2 %collective-permute-start = (bf16[4,128,256]{2,1,0:T(8,128)(2,1)S(1)}, bf16[4,128,256]{2,1,0:T(8,128)(2,1)S(1)}, u32[]{:S(2)}, u32[]{:S(2)}) collective-permute-start(bf16[4,128,256]{2,1,0:T(8,128)(2,1)S(1)} %bitcast.92), channel_id=1, source_target_pairs={{0,48},{1,16},{2,40},{3,8},{4,32},{5,0},{6,56},{7,24},{8,25},{9,57... | collective-permute-start | bytes 786440 | tf_op jit(solution)/shard_map/ppermute | solution.py:61
  18.7 6.0 %collective-permute-start.1 = (bf16[4,128,256]{2,1,0:T(8,128)(2,1)S(1)}, bf16[4,128,256]{2,1,0:T(8,128)(2,1)S(1)}, u32[]{:S(2)}, u32[]{:S(2)}) collective-permute-start(bf16[4,128,256]{2,1,0:T(8,128)(2,1)S(1)} %bitcast.93), channel_id=1, source_target_pairs={{0,112},{1,80},{2,104},{3,72},{4,96},{5,64},{6,120},{7,88},{8,89},... | collective-permute-start | bytes 786440 | tf_op jit(solution)/shard_map/ppermute | solution.py:61
  38.5 23.5 %all_to_all.45 = bf16[8,4,16,256]{3,2,1,0:T(8,128)(2,1)S(1)} all-to-all(bf16[8,4,16,256]{3,2,1,0:T(8,128)(2,1)S(1)} %diagonal0.1), channel_id=1, replica_groups=mesh['row'=32,'col'=8] {'col'}, dimensions={0} | all-to-all | bytes 524288 | tf_op jit(solution)/shard_map/all_to_all | solution.py:263
  66.9 34.4 %all_to_all.46.x_ref = bf16[32,4,16,256]{3,2,1,0:T(8,128)(2,1)S(1)} all-to-all(bf16[32,4,16,256]{3,2,1,0:T(8,128)(2,1)S(1)} %broadcast_in_dim.42), channel_id=1, replica_groups=mesh['row'=32,'col'=8] {'row'}, dimensions={0} | all-to-all | bytes 2097152 | tf_op jit(solution)/shard_map/all_to_all | solution.py:263
  101.3 3.7 %lower0.1 = bf16[8,4,16,256]{3,2,1,0:T(8,128)(2,1)} custom-call(s32[13]{0:T(128)S(1)} %concatenate.25.s, s32[128]{0:T(128)S(1)} %reshape.92.k, bf16[32,4,16,256]{3,2,1,0:T(8,128)(2,1)S(1)} %all_to_all.46.x_ref, bf16[2,4,256,256]{3,2,1,0:T(8,128)(2,1)S(1)} %bitcast.84, bf16[3,4,256,256]{3,2,1,0:T(8,128)(2,1)S(1)} %bitcast.86, ...), custom_call_target="tpu_custom_call" | custom-call | tf_op jit(solution)/shard_map/lower0/pallas_call | solution.py:133
  105.0 9.1 %all-to-all-start.2 = ((bf16[8,4,16,256]{3,2,1,0:T(8,128)(2,1)}), bf16[8,4,16,256]{3,2,1,0:T(8,128)(2,1)S(1)}, u32[]{:S(2)}, u32[]{:S(2)}) async-start(bf16[8,4,16,256]{3,2,1,0:T(8,128)(2,1)} %lower0.1), calls=%async_computation.2 | async-start | bytes 524288 | tf_op jit(solution)/shard_map/all_to_all | solution.py:263
  114.8 9.1 %all-to-all-done.2.x_ref = bf16[8,4,16,256]{3,2,1,0:T(8,128)(2,1)S(1)} async-done(((bf16[8,4,16,256]{3,2,1,0:T(8,128)(2,1)}), bf16[8,4,16,256]{3,2,1,0:T(8,128)(2,1)S(1)}, u32[]{:S(2)}, u32[]{:S(2)}) %all-to-all-start.2) | async-done | bytes 262176 | tf_op jit(solution)/shard_map/all_to_all | solution.py:263
  123.9 13.3 %all_to_all.47.refs_0_ = bf16[16,2,16,256]{3,2,1,0:T(8,128)(2,1)S(1)} all-to-all(bf16[16,2,16,256]{3,2,1,0:T(8,128)(2,1)S(1)} %get-tuple-element.41), channel_id=1, replica_groups={{0,8,16,24,32,40,48,56,64,72,80,88,96,104,112,120},{128,136,144,152,160..., dimensions={0} | all-to-all | bytes 524288 | tf_op jit(solution)/shard_map/all_to_all | solution.py:263
  137.3 4.2 %copy-done = bf16[8,10,256,256]{3,2,1,0:T(8,128)(2,1)S(1)} copy-done((bf16[8,10,256,256]{3,2,1,0:T(8,128)(2,1)S(1)}, bf16[8,10,256,256]{3,2,1,0:T(8,128)(2,1)}, u32[]{:S(2)}) %copy-start) | copy-done | bytes 10485784
  144.2 4.8 %all-to-all-start.4 = ((bf16[32,2,16,256]{3,2,1,0:T(8,128)(2,1)}), bf16[32,2,16,256]{3,2,1,0:T(8,128)(2,1)S(1)}, u32[]{:S(2)}, u32[]{:S(2)}) async-start(bf16[32,2,16,256]{3,2,1,0:T(8,128)(2,1)} %get-tuple-element.42), calls=%async_computation.4 | async-start | bytes 1048576 | tf_op jit(solution)/shard_map/all_to_all | solution.py:263
  149.8 13.9 %all-to-all-done.4.refs_0_ = bf16[32,2,16,256]{3,2,1,0:T(8,128)(2,1)S(1)} async-done(((bf16[32,2,16,256]{3,2,1,0:T(8,128)(2,1)}), bf16[32,2,16,256]{3,2,1,0:T(8,128)(2,1)S(1)}, u32[]{:S(2)}, u32[]{:S(2)}) %all-to-all-start.4) | async-done | bytes 524320 | tf_op jit(solution)/shard_map/all_to_all | solution.py:263
  163.6 4.0 %copy-done.1 = bf16[8,10,256,256]{3,2,1,0:T(8,128)(2,1)S(1)} copy-done((bf16[8,10,256,256]{3,2,1,0:T(8,128)(2,1)S(1)}, bf16[8,10,256,256]{3,2,1,0:T(8,128)(2,1)}, u32[]{:S(2)}) %copy-start.1) | copy-done | bytes 10485784
  167.6 3.3 %lower2.1 = (bf16[16,1,16,256]{3,2,1,0:T(8,128)(2,1)}, f32[1,16,256]{2,1,0:T(8,128)}) custom-call(s32[13]{0:T(128)S(1)} %concatenate.25.s, bf16[32,2,16,256]{3,2,1,0:T(8,128)(2,1)S(1)} %all-to-all-done.4.refs_0_, bf16[8,10,256,256]{3,2,1,0:T(8,128)(2,1)S(1)} %copy-done.1, f32[1,16,256]{2,1,0:T(8,128)S(1)} %get-tuple-element.43.refs_2_), custom_call_target="tpu_custom_call" | custom-call | flops 536870912 | bytes 4194304 | tf_op jit(solution)/shard_map/lower2/pallas_call | solution.py:203
  170.9 5.4 %all-to-all-start.5 = ((bf16[16,1,16,256]{3,2,1,0:T(8,128)(2,1)}), bf16[16,1,16,256]{3,2,1,0:T(8,128)(2,1)S(1)}, u32[]{:S(2)}, u32[]{:S(2)}) async-start(bf16[16,1,16,256]{3,2,1,0:T(8,128)(2,1)} %get-tuple-element.44), calls=%async_computation.5 | async-start | bytes 262144 | tf_op jit(solution)/shard_map/all_to_all | solution.py:263
  177.0 7.1 %all-to-all-done.5.refs_0_ = bf16[16,1,16,256]{3,2,1,0:T(8,128)(2,1)S(1)} async-done(((bf16[16,1,16,256]{3,2,1,0:T(8,128)(2,1)}), bf16[16,1,16,256]{3,2,1,0:T(8,128)(2,1)S(1)}, u32[]{:S(2)}, u32[]{:S(2)}) %all-to-all-start.5) | async-done | bytes 131104 | tf_op jit(solution)/shard_map/all_to_all | solution.py:263
  184.2 4.2 %copy-done.2 = bf16[8,10,256,256]{3,2,1,0:T(8,128)(2,1)S(1)} copy-done((bf16[8,10,256,256]{3,2,1,0:T(8,128)(2,1)S(1)}, bf16[8,10,256,256]{3,2,1,0:T(8,128)(2,1)}, u32[]{:S(2)}) %copy-start.2) | copy-done | bytes 10485784
  190.6 4.8 %all-to-all-start.6 = ((bf16[32,1,16,256]{3,2,1,0:T(8,128)(2,1)}), bf16[32,1,16,256]{3,2,1,0:T(8,128)(2,1)S(1)}, u32[]{:S(2)}, u32[]{:S(2)}) async-start(bf16[32,1,16,256]{3,2,1,0:T(8,128)(2,1)} %get-tuple-element.47), calls=%async_computation.6 | async-start | bytes 524288 | tf_op jit(solution)/shard_map/all_to_all | solution.py:263
  195.4 6.5 %all-gather.11.cloned.1.call-done = bf16[32,256,256]{2,1,0:T(8,128)(2,1)} async-done(((bf16[4,256,256]{2,1,0:T(8,128)(2,1)}), bf16[32,256,256]{2,1,0:T(8,128)(2,1)}) %all-gather.11.cloned.1.call-update) | async-done | bytes 4194320 | tf_op jit(solution)/shard_map/all_gather | solution.py:330
  202.6 3.2 %all-to-all-done.6.refs_2_ = bf16[32,1,16,256]{3,2,1,0:T(8,128)(2,1)S(1)} async-done(((bf16[32,1,16,256]{3,2,1,0:T(8,128)(2,1)}), bf16[32,1,16,256]{3,2,1,0:T(8,128)(2,1)S(1)}, u32[]{:S(2)}, u32[]{:S(2)}) %all-to-all-start.6) | async-done | bytes 262176 | tf_op jit(solution)/shard_map/all_to_all | solution.py:263
  205.9 4.6 %copy-done.3 = bf16[8,12,256,256]{3,2,1,0:T(8,128)(2,1)S(1)} copy-done((bf16[8,12,256,256]{3,2,1,0:T(8,128)(2,1)S(1)}, bf16[8,12,256,256]{3,2,1,0:T(8,128)(2,1)}, u32[]{:S(2)}) %copy-start.3) | copy-done | bytes 12582936
  210.4 6.0 %lower3.1 = (bf16[32,1,16,256]{3,2,1,0:T(8,128)(2,1)S(1)}, f32[1,16,256]{2,1,0:T(8,128)}) custom-call(s32[13]{0:T(128)S(1)} %concatenate.25.s, bf16[32,2,16,256]{3,2,1,0:T(8,128)(2,1)S(1)} %all-to-all-done.4.refs_0_, bf16[8,12,256,256]{3,2,1,0:T(8,128)(2,1)S(1)} %copy-done.3, bf16[32,1,16,256]{3,2,1,0:T(8,128)(2,1)S(1)} %all-to-all-done.6.refs_2_, ...), custom_call_target="tpu_custom_call" | custom-call | flops 1610612736 | bytes 12582912 | tf_op jit(solution)/shard_map/lower3/pallas_call | solution.py:203
  216.4 16.6 %all_to_all.48.refs_0_ = bf16[32,1,16,256]{3,2,1,0:T(8,128)(2,1)S(1)} all-to-all(bf16[32,1,16,256]{3,2,1,0:T(8,128)(2,1)S(1)} %get-tuple-element.50), channel_id=1, replica_groups=mesh['row'=32,'col'=8] {'row'}, dimensions={0} | all-to-all | bytes 524288 | tf_op jit(solution)/shard_map/all_to_all | solution.py:263
  233.0 3.2 %diagonal3.1 = (bf16[1,1,16,256]{3,2,1,0:T(8,128)(2,1)}, f32[1,16,256]{2,1,0:T(8,128)S(1)}) custom-call(s32[13]{0:T(128)S(1)} %concatenate.25.s, bf16[32,1,16,256]{3,2,1,0:T(8,128)(2,1)S(1)} %all_to_all.48.refs_0_, bf16[8,4,256,256]{3,2,1,0:T(8,128)(2,1)S(1)} %bitcast.82), custom_call_target="tpu_custom_call" | custom-call | flops 536870912 | bytes 4194304 | tf_op jit(solution)/shard_map/diagonal3/pallas_call | solution.py:203
  237.0 6.7 %all-to-all-start.8 = ((f32[8,2,16,256]{3,2,1,0:T(8,128)}), f32[8,2,16,256]{3,2,1,0:T(8,128)S(1)}, u32[]{:S(2)}, u32[]{:S(2)}) async-start(f32[8,2,16,256]{3,2,1,0:T(8,128)} %broadcast_in_dim.49), calls=%async_computation.8 | async-start | bytes 524288 | tf_op jit(solution)/shard_map/all_to_all | solution.py:263
  (77 shorter events, 41.7 us)
Async XLA Ops:
  6.5 8.3 %slice-start = ((bf16[7,1,256,2,1,256]{5,3,4,2,1,0:T(2,128)(2,1)}), bf16[1,1,256,2,1,256]{5,3,4,2,1,0:T(2,128)(2,1)S(1)}, s32[]{:S(2)}) async-start(bf16[7,1,256,2,1,256]{5,3,4,2,1,0:T(2,128)(2,1)} %param.9), calls=%async_computation.13 | async-start | bytes 524288 | tf_op jit(solution)/shard_map/slice | solution.py:319
  6.5 107.6 %all-gather.7.cloned.1.call-start = ((), (), s32[]{:S(2)}) async-start(), calls=%async_computation.9 | async-start | bytes 11796480 | tf_op jit(solution)/shard_map/all_gather | solution.py:323
  7.8 8.3 %collective-permute-start = (bf16[4,128,256]{2,1,0:T(8,128)(2,1)S(1)}, bf16[4,128,256]{2,1,0:T(8,128)(2,1)S(1)}, u32[]{:S(2)}, u32[]{:S(2)}) collective-permute-start(bf16[4,128,256]{2,1,0:T(8,128)(2,1)S(1)} %bitcast.92), channel_id=1, source_target_pairs={{0,48},{1,16},{2,40},{3,8},{4,32},{5,0},{6,56},{7,24},{8,25},{9,57... | collective-permute-start | bytes 786440 | tf_op jit(solution)/shard_map/ppermute | solution.py:61
  18.6 157.7 %all-gather.9.cloned.1.call-start = ((), (), s32[]{:S(2)}) async-start(), calls=%async_computation.10 | async-start | bytes 14155776 | tf_op jit(solution)/shard_map/all_gather | solution.py:329
  18.7 10.1 %collective-permute-start.1 = (bf16[4,128,256]{2,1,0:T(8,128)(2,1)S(1)}, bf16[4,128,256]{2,1,0:T(8,128)(2,1)S(1)}, u32[]{:S(2)}, u32[]{:S(2)}) collective-permute-start(bf16[4,128,256]{2,1,0:T(8,128)(2,1)S(1)} %bitcast.93), channel_id=1, source_target_pairs={{0,112},{1,80},{2,104},{3,72},{4,96},{5,64},{6,120},{7,88},{8,89},... | collective-permute-start | bytes 786440 | tf_op jit(solution)/shard_map/ppermute | solution.py:61
  30.1 1.0 copy-start.8
  30.1 171.8 %all-gather.11.cloned.1.call-start = ((), (), s32[]{:S(2)}) async-start(), calls=%async_computation.11 | async-start | bytes 4718592 | tf_op jit(solution)/shard_map/all_gather | solution.py:330
  32.1 1.2 slice-start.1
  32.1 1.4 slice-start.2
  37.5 63.9 %copy-start.6 = (bf16[1,1,256,12,1,256]{5,2,4,3,1,0:T(8,128)(2,1)S(1)}, bf16[1,1,256,12,1,256]{5,2,4,3,1,0:T(8,128)(2,1)}, u32[]{:S(2)}) copy-start(bf16[1,1,256,12,1,256]{5,2,4,3,1,0:T(8,128)(2,1)} %param.12) | copy-start | bytes 4718596
  38.5 62.8 %copy-start.4 = (bf16[1,1,256,28,1,256]{5,2,4,3,1,0:T(8,128)(2,1)S(1)}, bf16[1,1,256,28,1,256]{5,2,4,3,1,0:T(8,128)(2,1)}, u32[]{:S(2)}) copy-start(bf16[1,1,256,28,1,256]{5,2,4,3,1,0:T(8,128)(2,1)} %param.13) | copy-start | bytes 11010052
  62.1 4.7 %collective-permute-start.2 = (bf16[4,16,256]{2,1,0:T(8,128)(2,1)S(1)}, bf16[4,16,256]{2,1,0:T(8,128)(2,1)S(1)}, u32[]{:S(2)}, u32[]{:S(2)}) collective-permute-start(bf16[4,16,256]{2,1,0:T(8,128)(2,1)S(1)} %convert_element_type.25), channel_id=1, source_target_pairs={{0,48},{1,16},{2,40},{3,8},{4,32},{5,0},{6,56},{7,24},{8,25},{9,57... | collective-permute-start | bytes 98312 | tf_op jit(solution)/shard_map/ppermute | solution.py:61
  105.0 18.8 %all-to-all-start.2 = ((bf16[8,4,16,256]{3,2,1,0:T(8,128)(2,1)}), bf16[8,4,16,256]{3,2,1,0:T(8,128)(2,1)S(1)}, u32[]{:S(2)}, u32[]{:S(2)}) async-start(bf16[8,4,16,256]{3,2,1,0:T(8,128)(2,1)} %lower0.1), calls=%async_computation.2 | async-start | bytes 524288 | tf_op jit(solution)/shard_map/all_to_all | solution.py:263
  137.3 4.2 %copy-start = (bf16[8,10,256,256]{3,2,1,0:T(8,128)(2,1)S(1)}, bf16[8,10,256,256]{3,2,1,0:T(8,128)(2,1)}, u32[]{:S(2)}) copy-start(bf16[8,10,256,256]{3,2,1,0:T(8,128)(2,1)} %all-gather.7.cloned.1.call-done.refs_1_) | copy-start | bytes 31457284
  144.2 19.4 %all-to-all-start.4 = ((bf16[32,2,16,256]{3,2,1,0:T(8,128)(2,1)}), bf16[32,2,16,256]{3,2,1,0:T(8,128)(2,1)S(1)}, u32[]{:S(2)}, u32[]{:S(2)}) async-start(bf16[32,2,16,256]{3,2,1,0:T(8,128)(2,1)} %get-tuple-element.42), calls=%async_computation.4 | async-start | bytes 1048576 | tf_op jit(solution)/shard_map/all_to_all | solution.py:263
  149.0 94.6 %all-gather.13.cloned.1.call-start = ((), (), s32[]{:S(2)}) async-start(), calls=%async_computation.12 | async-start | bytes 1179648 | tf_op jit(solution)/shard_map/all_gather | solution.py:347
  163.6 4.0 %copy-start.1 = (bf16[8,10,256,256]{3,2,1,0:T(8,128)(2,1)S(1)}, bf16[8,10,256,256]{3,2,1,0:T(8,128)(2,1)}, u32[]{:S(2)}) copy-start(bf16[8,10,256,256]{3,2,1,0:T(8,128)(2,1)} %all-gather.7.cloned.1.call-done.refs_1_) | copy-start | bytes 31457284
  170.9 13.3 %all-to-all-start.5 = ((bf16[16,1,16,256]{3,2,1,0:T(8,128)(2,1)}), bf16[16,1,16,256]{3,2,1,0:T(8,128)(2,1)S(1)}, u32[]{:S(2)}, u32[]{:S(2)}) async-start(bf16[16,1,16,256]{3,2,1,0:T(8,128)(2,1)} %get-tuple-element.44), calls=%async_computation.5 | async-start | bytes 262144 | tf_op jit(solution)/shard_map/all_to_all | solution.py:263
  184.2 4.2 %copy-start.2 = (bf16[8,10,256,256]{3,2,1,0:T(8,128)(2,1)S(1)}, bf16[8,10,256,256]{3,2,1,0:T(8,128)(2,1)}, u32[]{:S(2)}) copy-start(bf16[8,10,256,256]{3,2,1,0:T(8,128)(2,1)} %all-gather.7.cloned.1.call-done.refs_1_) | copy-start | bytes 31457284
  190.6 15.2 %all-to-all-start.6 = ((bf16[32,1,16,256]{3,2,1,0:T(8,128)(2,1)}), bf16[32,1,16,256]{3,2,1,0:T(8,128)(2,1)S(1)}, u32[]{:S(2)}, u32[]{:S(2)}) async-start(bf16[32,1,16,256]{3,2,1,0:T(8,128)(2,1)} %get-tuple-element.47), calls=%async_computation.6 | async-start | bytes 524288 | tf_op jit(solution)/shard_map/all_to_all | solution.py:263
  205.8 4.6 %copy-start.3 = (bf16[8,12,256,256]{3,2,1,0:T(8,128)(2,1)S(1)}, bf16[8,12,256,256]{3,2,1,0:T(8,128)(2,1)}, u32[]{:S(2)}) copy-start(bf16[8,12,256,256]{3,2,1,0:T(8,128)(2,1)} %all-gather.9.cloned.1.call-done.refs_1_.refs_3_) | copy-start | bytes 37748740
  210.4 22.6 %copy-start.5 = (bf16[32,256,256]{2,1,0:T(8,128)(2,1)S(1)}, bf16[32,256,256]{2,1,0:T(8,128)(2,1)}, u32[]{:S(2)}) copy-start(bf16[32,256,256]{2,1,0:T(8,128)(2,1)} %all-gather.11.cloned.1.call-done) | copy-start | bytes 12582916
  237.0 13.2 %all-to-all-start.8 = ((f32[8,2,16,256]{3,2,1,0:T(8,128)}), f32[8,2,16,256]{3,2,1,0:T(8,128)S(1)}, u32[]{:S(2)}, u32[]{:S(2)}) async-start(f32[8,2,16,256]{3,2,1,0:T(8,128)} %broadcast_in_dim.49), calls=%async_computation.8 | async-start | bytes 524288 | tf_op jit(solution)/shard_map/all_to_all | solution.py:263
  243.6 1.2 copy-start.7
Sparse Core Ops, SparseCore 0:
  18.7 71.3 all-gather.6
  91.9 73.0 all-gather.8
  166.8 35.0 all-gather.10
  203.6 25.8 all-gather.12

commit v2 on v1

--- a/solution.py
+++ b/solution.py
@@ -69,29 +69,36 @@
     return lax.dynamic_index_in_dim(array, index, axis, keepdims=False)
 
 
-def params():
-    return pltpu.CompilerParams(vmem_limit_bytes=24 * 1024 * 1024)
+def params(mib=24):
+    return pltpu.CompilerParams(vmem_limit_bytes=mib * 1024 * 1024)
 
 
 def whole(*_):
     return pl.BlockSpec(memory_space=pltpu.VMEM)
 
 
-def diagonal0(place, near, far, tiles):
-    def kernel(s, near_ref, far_ref, tile_ref, out_ref):
-        e = s[1]
+def diagonal0(place, near, far, tiles, ready, passed):
+    count = len(ready)
+
+    def kernel(s, near_ref, far_ref, tile_ref, *refs):
+        e, out_ref = s[1], refs[count + len(passed)]
         for a in range(4):
-            value = dot(tile_ref[a, e], near_ref[a]) + dot(tile_ref[a, 1 - e], far_ref[a])
+            value = jnp.dot(tile_ref[a, e], near_ref[a], preferred_element_type=F32)
+            value += jnp.dot(tile_ref[a, 1 - e], far_ref[a], preferred_element_type=F32)
             out_ref[:, a] = value.T.reshape(8, 16, 256).astype(BF)
 
-    return pl.pallas_call(
-        kernel,
-        out_shape=jax.ShapeDtypeStruct((8, 4, 16, 256), BF),
-        in_specs=[pl.BlockSpec(memory_space=pltpu.SMEM), whole(), whole(), whole()],
-        out_specs=whole(),
+    anywhere = pl.BlockSpec(memory_space=pl.ANY)
+    return pl.pallas_call(
+        kernel,
+        out_shape=(jax.ShapeDtypeStruct((8, 4, 16, 256), BF),)
+        + tuple(jax.ShapeDtypeStruct(value.shape, value.dtype) for value in passed),
+        in_specs=[pl.BlockSpec(memory_space=pltpu.SMEM), whole(), whole(), whole()]
+        + [anywhere] * (count + len(passed)),
+        out_specs=(whole(),) + (anywhere,) * len(passed),
+        input_output_aliases={4 + count + i: 1 + i for i in range(len(passed))},
         compiler_params=params(),
         name="diagonal0",
-    )(place, near, far, tiles)
+    )(place, near, far, tiles, *ready, *passed)
 
 
 def lower0(place, keep, slices, one, two, last):
@@ -102,7 +109,7 @@
             tiles = jnp.concatenate([tile for _, tile, _ in pairs], axis=1)
             blocks = []
             for a0, _, flag in pairs:
-                block = jnp.concatenate([x_ref[p, a0] for p in range(8)], axis=0)
+                block = jnp.concatenate([x_ref[p % 4, p // 4, a0] for p in range(8)], axis=0)
                 blocks.append(jnp.where(flag != 0, block, jnp.zeros_like(block)))
             return dot(tiles, jnp.concatenate(blocks, axis=1))
 
@@ -137,7 +144,7 @@
             num_scalar_prefetch=2,
             grid=(4,),
             in_specs=[
-                pl.BlockSpec((8, 4, 16, 256), lambda c, s, k: (c, 0, 0, 0)),
+                pl.BlockSpec((4, 2, 4, 16, 256), lambda c, s, k: (0, c, 0, 0, 0)),
                 pl.BlockSpec((2, 1, 256, 256), lambda c, s, k: (0, c, 0, 0)),
                 pl.BlockSpec((2, 1, 256, 256), lambda c, s, k: (0, c, 0, 0)),
                 pl.BlockSpec((4, 1, 256, 256), lambda c, s, k: (0, c, 0, 0)),
@@ -150,8 +157,11 @@
     )(place, keep, slices, one, two, last)
 
 
-def multiply(place, terms, base, n_out, copies, dtype, name, token=None):
+def multiply(place, terms, base, n_out, copies, name, dtype=BF, early=None):
     steps = terms[0][3]
+    early = early or ()
+    lead = sum(value.shape[0] for value in early)
+    total = n_out if not early else 8
 
     def kernel(s, *refs):
         step = pl.program_id(0)
@@ -181,10 +191,14 @@
                 value = acc[o].T
                 if base is not None:
                     value = refs[2 * len(terms)][o] - value
-                out_ref[o] = value
+                out_ref[lead + o] = value
                 cast = value.astype(dtype)
                 for r in range(copies):
                     copy_ref[r, o] = cast
+            if early:
+                out_ref[0:4] = refs[2 * len(terms)][...]
+                out_ref[4:6] = refs[2 * len(terms) + 1][...]
+                out_ref[7:8] = jnp.zeros((1, 16, 256), F32)
 
     args, specs, size = [], [], 0
     for x, tiles, first, _, count, _ in terms:
@@ -197,14 +211,14 @@
     if base is not None:
         args.append(base)
         specs.append(pl.BlockSpec(base.shape, lambda i, s: (0, 0, 0)))
-    if token is not None:
-        args.append(token)
-        specs.append(pl.BlockSpec(token.shape, lambda i, s: (0, 0)))
+    for value in early:
+        args.append(value)
+        specs.append(pl.BlockSpec(value.shape, lambda i, s: (0, 0, 0)))
     return pl.pallas_call(
         kernel,
         out_shape=(
             jax.ShapeDtypeStruct((copies, n_out, 16, 256), dtype),
-            jax.ShapeDtypeStruct((n_out, 16, 256), F32),
+            jax.ShapeDtypeStruct((total, 16, 256), F32),
         ),
         grid_spec=pltpu.PrefetchScalarGridSpec(
             num_scalar_prefetch=1,
@@ -212,7 +226,7 @@
             in_specs=specs,
             out_specs=(
                 pl.BlockSpec((copies, n_out, 16, 256), lambda i, s: (0, 0, 0, 0)),
-                pl.BlockSpec((n_out, 16, 256), lambda i, s: (0, 0, 0)),
+                pl.BlockSpec((total, 16, 256), lambda i, s: (0, 0, 0)),
             ),
             scratch_shapes=[pltpu.VMEM((n_out, 256, 16), F32)],
         ),
@@ -229,7 +243,7 @@
     return pl.pallas_call(
         kernel,
         out_shape=jax.ShapeDtypeStruct((8, 256, 128), F32),
-        grid=(6,),
+        grid=(7,),
         in_specs=[pl.BlockSpec((8, 1, 16, 256), lambda i: (0, i, 0, 0))],
         out_specs=pl.BlockSpec((1, 256, 128), lambda i: (i, 0, 0)),
         compiler_params=params(),
@@ -244,12 +258,12 @@
     return pl.pallas_call(
         kernel,
         out_shape=jax.ShapeDtypeStruct((8, 256, 128), F32),
-        grid=(2,),
+        grid=(1,),
         in_specs=[
             pl.BlockSpec((8, 1, 16, 256), lambda i: (0, i, 0, 0)),
             pl.BlockSpec(memory_space=pl.ANY),
         ],
-        out_specs=pl.BlockSpec((1, 256, 128), lambda i: (6 + i, 0, 0)),
+        out_specs=pl.BlockSpec((1, 256, 128), lambda i: (7 + i, 0, 0)),
         input_output_aliases={1: 0},
         compiler_params=params(),
         name="assemble_late",
@@ -257,6 +271,8 @@
 
 
 HALVES = [list(range(16)), list(range(16, 32))]
+ALONG_Z = [[4 * z + x for z in range(8)] for x in range(4)]
+ALONG_X = [[4 * z + x for x in range(4)] for z in range(8)]
 
 
 def exchange(copies, axis, groups=None):
@@ -267,8 +283,8 @@
     return send(value, [(i, i ^ mask) for i in range(256)])
 
 
-def finish0(sums, upper, token):
-    def kernel(x_ref, upper_ref, _, copy_ref, two_ref, three_ref):
+def finish0(sums, upper):
+    def kernel(x_ref, upper_ref, copy_ref, two_ref, three_ref):
         value = upper_ref[...] - jnp.sum(x_ref[...].astype(F32), axis=0)
         two_ref[...] = value[2:3]
         three_ref[...] = value[3:4]
@@ -282,11 +298,7 @@
         out_shape=(jax.ShapeDtypeStruct((16, 2, 16, 256), BF), slot, slot),
         compiler_params=params(),
         name="finish0",
-    )(sums, upper, token)
-
-
-def arrived(tiles):
-    return tiles[0, 0, 0:16, 0:128]
+    )(sums, upper)
 
 
 def body(rhs, inverse_low, inverse_top, lower_one, lower_two, lower_top, block_rows):
@@ -298,62 +310,57 @@
     place = jnp.concatenate(
         [jnp.stack([m, e, core, h]), at(jnp.array(owner, jnp.int32), col), col[None]]
     ).astype(jnp.int32)
-    sent0 = jnp.swapaxes(rhs[0:4, 0], 1, 2).astype(BF)
+    sent0 = rhs[0:4, 0].astype(BF)
     near = send(sent0, spread_pairs(0))
     far = send(sent0, spread_pairs(1))
 
     lists = at(block_rows.reshape(32, 8, 64), col, 1)
-    targets = jnp.stack([128 + row, 160 + row, 192 + row, 224 + row])
-    listed = jnp.any(lists[None] == targets[:, None, None], axis=-1)
-    keep = listed.astype(jnp.int32).reshape(128)
+
+    def listed(block_row, first, count):
+        return jnp.any(lax.dynamic_slice(lists, (first, 0), (count, 64)) == block_row, axis=-1)
 
     def masked(tiles, flags):
         return jnp.where(flags[:, None, None], tiles, jnp.zeros_like(tiles))
 
+    low = lax.optimization_barrier(jnp.swapaxes(inverse_low[:, 0, :, :, 0, :], 1, 2))
     two = jnp.swapaxes(lower_two[0, 0, :, :, 0, :], 0, 1).reshape(3, 4, 256, 256)
     last = jnp.swapaxes(lower_top[0, 0, :, :, 0, :], 0, 1).reshape(7, 4, 256, 256)
-    first = jnp.concatenate(
-        [
-            jnp.swapaxes(inverse_low[4:6, 0, :, :, 0, :], 1, 2).reshape(4, 256, 256),
-            masked(two[2], lax.dynamic_slice(listed[2], (16 + 4 * h,), (4,))),
-            jnp.swapaxes(inverse_low[6, 0, :, :, 0, :], 0, 1),
-        ]
-    )
-    gate = near[0, 0, 0] * 0
-    first = lax.all_gather(first + gate, "col")
-    low, one, upper = lax.optimization_barrier((inverse_low[0:4], lower_one, rhs[4:8, 0]))
-    low = jnp.swapaxes(low[:, 0, :, :, 0, :], 1, 2)
-    one = jnp.swapaxes(one[:, 0, :, :, 0, :], 1, 2)
-    upper = lax.dynamic_slice(jnp.swapaxes(upper, 1, 2), (0, 16 * col, 0), (4, 16, 256))
-    near, far, last_later, inverse_top = lax.optimization_barrier((near, far, last[4:7], inverse_top))
-    second = lax.all_gather(masked(last_later.reshape(12, 256, 256), listed[3, 16:28]) + gate, "col")
-    third = lax.all_gather(jnp.swapaxes(inverse_top[0, 0, :, :, 0, :], 0, 1) + gate, "col")
-
-    near, far, keep, upper, one = lax.optimization_barrier((near, far, keep, upper, one))
-
-    sums = exchange(diagonal0(place, near, far, low), "col")
+    low1, low2 = low[4:6].reshape(4, 256, 256), low[6]
+    two1 = masked(two[2], listed(192 + row, 16 + 4 * h, 4))
+    first = lax.all_gather(jnp.concatenate([low1, two1, low2]), "col")
+    one = jnp.swapaxes(lower_one[:, 0, :, :, 0, :], 1, 2)
+    upper = lax.dynamic_slice(jnp.swapaxes(rhs[4:8, 0], 1, 2), (0, 16 * col, 0), (4, 16, 256))
+    targets = jnp.stack([128 + row, 160 + row, 192 + row, 224 + row])
+    keep = jnp.any(lists[None] == targets[:, None, None], axis=-1).astype(jnp.int32).reshape(128)
+
+    second = masked(last[4:7].reshape(12, 256, 256), listed(224 + row, 16, 12))
+    third = jnp.swapaxes(inverse_top[0, 0, :, :, 0, :], 0, 1)
+
+    part, second, third = diagonal0(place, near, far, low[0:4], (one, upper, keep), (second, third))
+    second, third = [lax.all_gather(value, "col") for value in (second, third)]
+    sums = exchange(part, "col")
     solved0 = jnp.sum(sums.astype(F32), axis=0)
     slices = send(solved0.astype(BF), turn_pairs())
-    slices, one = lax.optimization_barrier((slices, one))
-    slices = exchange(jnp.broadcast_to(slices, (32, 4, 16, 256)), "row")
+    slices = exchange(jnp.broadcast_to(slices, (8, 4, 16, 256)), "row", ALONG_Z)
+    slices = exchange(jnp.broadcast_to(slices, (4, 8, 4, 16, 256)), "row", ALONG_X)
     sums = exchange(lower0(place, keep, slices, one, two, last), "col")
-    copies, base2, base3 = finish0(sums, upper, arrived(first))
+    copies, base2, base3 = finish0(sums, upper)
 
     reduced = exchange(copies, "row", HALVES)
     copies, solved1 = multiply(
-        place, [(reduced, first, 0, 1, 4, lambda i, h: [(t, t % 2, t // 2, t // 2) for t in range(4)])], None, 2, 32, BF, "diagonal1"
+        place, [(reduced, first, 0, 1, 4, lambda i, h: [(t, t % 2, t // 2, t // 2) for t in range(4)])], None, 2, 32, "diagonal1"
     )
     x1 = exchange(copies, "row")
-    early = lax.all_gather(jnp.concatenate([solved0, solved1, solved1]), "col")
 
     copies, _ = multiply(
-        place, [(x1, first, 4, 4, 1, lambda i, h: [(0, i, h, 0)])], base2, 1, 16, BF, "lower2"
+        place, [(x1, first, 4, 4, 1, lambda i, h: [(0, i, h, 0)])], base2, 1, 16, "lower2"
     )
     reduced = exchange(copies, "row", HALVES)
     copies, solved2 = multiply(
-        place, [(reduced, first, 8, 2, 1, lambda i, h: [(0, i, 0, 0)])], None, 1, 32, BF, "diagonal2", arrived(second)
+        place, [(reduced, first, 8, 2, 1, lambda i, h: [(0, i, 0, 0)])], None, 1, 32, "diagonal2", early=(solved0, solved1)
     )
     x2 = exchange(copies, "row")
+    early = lax.all_gather(solved2, "col")
 
     copies, _ = multiply(
         place,
@@ -361,14 +368,13 @@
             (x1, second, 0, 4, 2, lambda i, h: [(t, (2 * i + t) % 4, i // 2, 0) for t in range(2)]),
             (x2, second, 8, 4, 1, lambda i, h: [(0, i, 0, 0)]),
         ],
-        base3, 1, 32, BF, "lower3", arrived(third),
+        base3, 1, 32, "lower3",
     )
     reduced = exchange(copies, "row")
-    _, solved3 = multiply(
-        place, [(reduced, third, 0, 4, 1, lambda i, h: [(0, i, 0, 0)])], None, 1, 1, BF, "diagonal3"
-    )
-    late = jnp.concatenate([solved2, solved3])
-    late = exchange(jnp.broadcast_to(late, (8, 2, 16, 256)), "col")
+    copies, _ = multiply(
+        place, [(reduced, third, 0, 4, 1, lambda i, h: [(0, i, 0, 0)])], None, 1, 8, "diagonal3", dtype=F32
+    )
+    late = exchange(copies, "col")
     return assemble_late(assemble_early(early), late)[:, None]
 
 

time: 259 us -> 240 us (0.927)
  blocking collectives: 87.9 us -> 130 us
  waiting for transfers between devices: 47.9 us -> 13.5 us
  starting transfers between devices: 43.2 us -> 27 us
  local copies, waits for them, and re-layouts: 33.3 us -> 23.8 us
    all_to_all x4 -> x8, blocking collectives: 87.9 us -> 130 us  [exchange(): lax.all_to_all(copies, axis, 0, 0, tiled=True, axis_index_groups=groups)]
    all_to_all x5 -> x2, waiting for transfers between devices: 36.2 us -> 11.4 us  [exchange(): lax.all_to_all(copies, axis, 0, 0, tiled=True, axis_index_groups=groups)]
    all_to_all x5 -> x2, starting transfers between devices: 30.7 us -> 12.2 us  [exchange(): lax.all_to_all(copies, axis, 0, 0, tiled=True, axis_index_groups=groups)]
    all_gather x4, waiting for transfers between devices: 6.55 us -> 0.03 us  [the longest x2 0.02 us: body(): second, third = [lax.all_gather(value, 'col') for value in (second, third)]]
    select_n x0 -> x2, other arithmetic: none -> 4.04 us  [masked(): return jnp.where(flags[:, None, None], tiles, jnp.zeros_like(tiles))]
    ppermute x3, waiting for transfers between devices: 5.11 us -> 1.37 us  [send(): return lax.ppermute(value, AXES, pairs)]
    add x3 -> x0, other arithmetic: 3.52 us -> none  [the longest x1 1.34 us: body(): masked(last_later.reshape(12, 256, 256), listed[3, 16:28]) + gate]
    unnamed x22 -> x26, local copies, waits for them, and re-layouts: 21.3 us -> 18.1 us
  transfers between devices with their start and end apart: 12 -> 9, of which waited for: 8 -> 4; matrix products, arithmetic and copies ran while one was open for 6% -> 4% of each run, Pallas kernels for 10% -> 10%
where the time goes in v2:
time: 240 us; the launch traced here: 239 us
  blocking collectives  130 us (54%)
  starting transfers between devices  27 us (11%)
  Pallas kernels  24.8 us (10%)
  local copies, waits for them, and re-layouts  23.8 us (10%)
  waiting for transfers between devices  13.5 us (6%)
  between operations  13.4 us (6%)
  other arithmetic  6.97 us (3%)
    all_to_all x8, blocking collectives, exchange(): lax.all_to_all(copies, axis, 0, 0, tiled=True, axis_index_groups=groups)  130 us
    unnamed x26, local copies, waits for them, and re-layouts  18.1 us
    pallas_call x5, Pallas kernels, multiply(): pl.pallas_call(kernel, out_shape=(jax.ShapeDtypeStruct((copies, n_out, 16...  16.8 us
    ppermute x3, starting transfers between devices, send(): return lax.ppermute(value, AXES, pairs)  14.7 us
    all_to_all x2, starting transfers between devices, exchange(): lax.all_to_all(copies, axis, 0, 0, tiled=True, axis_index_groups=groups)  12.2 us
    all_to_all x2, waiting for transfers between devices, exchange(): lax.all_to_all(copies, axis, 0, 0, tiled=True, axis_index_groups=groups)  11.4 us
  transfers between devices with their start and end apart: 9, of which 4 were waited for; matrix products, arithmetic and copies ran while one was open for 4% of the time, Pallas kernels for 10%

profile of v2, /device:TPU:1, one launch (start us, length us, event | category | flops | bytes accessed | tf_op | source)
XLA Modules:
  0.0 239.0 jit_solution(16617695947067880078)
XLA Ops:
  6.5 3.0 %copy.42 = bf16[7,1,256,2,1,256]{5,2,3,0,4,1:T(8,128)(2,1)} copy(bf16[7,1,256,2,1,256]{5,3,4,2,1,0:T(2,128)(2,1)} %param.9) | data formatting | bytes 3670016 | tf_op args[1]
  14.8 4.2 %collective-permute-start = (bf16[4,256,128]{2,1,0:T(8,128)(2,1)S(1)}, bf16[4,256,128]{2,1,0:T(8,128)(2,1)S(1)}, u32[]{:S(2)}, u32[]{:S(2)}) collective-permute-start(bf16[4,256,128]{2,1,0:T(8,128)(2,1)S(1)} %fusion), channel_id=1, source_target_pairs={{0,48},{1,16},{2,40},{3,8},{4,32},{5,0},{6,56},{7,24},{8,25},{9,57... | collective-permute-start | bytes 786440 | tf_op jit(solution)/shard_map/ppermute | solution.py:61
  19.0 5.6 %collective-permute-start.1 = (bf16[4,256,128]{2,1,0:T(8,128)(2,1)S(1)}, bf16[4,256,128]{2,1,0:T(8,128)(2,1)S(1)}, u32[]{:S(2)}, u32[]{:S(2)}) collective-permute-start(bf16[4,256,128]{2,1,0:T(8,128)(2,1)S(1)} %fusion), channel_id=1, source_target_pairs={{0,112},{1,80},{2,104},{3,72},{4,96},{5,64},{6,120},{7,88},{8,89},... | collective-permute-start | bytes 786440 | tf_op jit(solution)/shard_map/ppermute | solution.py:61
  31.8 2.9 %slice_select_fusion.refs_3_ = bf16[12,256,256]{2,1,0:T(8,128)(2,1)} fusion(bf16[28,256,256]{2,1,0:T(8,128)(2,1)} %bitcast.61, pred[12]{0:T(512)(128)(4,1)S(1)} %compare_reduce_fusion.1), kind=kLoop, calls=%fused_computation.1 | loop fusion | flops 786432 | bytes 3145740 | tf_op jit(solution)/shard_map/jit(_where)/select_n | solution.py:323
  36.9 15.4 %all_to_all.50 = bf16[8,4,16,256]{3,2,1,0:T(8,128)(2,1)S(1)} all-to-all(bf16[8,4,16,256]{3,2,1,0:T(8,128)(2,1)S(1)} %get-tuple-element.18), channel_id=1, replica_groups=mesh['row'=32,'col'=8] {'col'}, dimensions={0} | all-to-all | bytes 524288 | tf_op jit(solution)/shard_map/all_to_all | solution.py:279
  52.3 4.9 %collective-permute-start.2 = (bf16[4,16,256]{2,1,0:T(8,128)(2,1)S(1)}, bf16[4,16,256]{2,1,0:T(8,128)(2,1)S(1)}, u32[]{:S(2)}, u32[]{:S(2)}) collective-permute-start(bf16[4,16,256]{2,1,0:T(8,128)(2,1)S(1)} %convert_element_type.21), channel_id=1, source_target_pairs={{0,48},{1,16},{2,40},{3,8},{4,32},{5,0},{6,56},{7,24},{8,25},{9,57... | collective-permute-start | bytes 98312 | tf_op jit(solution)/shard_map/ppermute | solution.py:61
  58.2 18.7 %all_to_all.51 = bf16[8,4,16,256]{3,2,1,0:T(8,128)(2,1)S(1)} all-to-all(bf16[8,4,16,256]{3,2,1,0:T(8,128)(2,1)S(1)} %broadcast_in_dim.41), channel_id=1, replica_groups={{0,32,64,96,128,160,192,224},{8,40,72,104,136,168,200,232},{16,48,80,11..., dimensions={0} | all-to-all | bytes 524288 | tf_op jit(solution)/shard_map/all_to_all | solution.py:279
  77.0 17.5 %all_to_all.52.x_ref = bf16[4,8,4,16,256]{4,3,2,1,0:T(8,128)(2,1)S(1)} all-to-all(bf16[4,8,4,16,256]{4,3,2,1,0:T(8,128)(2,1)S(1)} %broadcast_in_dim.42), channel_id=1, replica_groups={{0,8,16,24},{32,40,48,56},{64,72,80,88},{96,104,112,120},{128,136,144,1..., dimensions={0} | all-to-all | bytes 2097152 | tf_op jit(solution)/shard_map/all_to_all | solution.py:279
  94.5 3.1 %lower0.1 = bf16[8,4,16,256]{3,2,1,0:T(8,128)(2,1)S(1)} custom-call(s32[13]{0:T(128)S(1)} %concatenate.6.s, s32[128]{0:T(128)S(1)} %reshape.41.refs_2_.k, bf16[4,8,4,16,256]{4,3,2,1,0:T(8,128)(2,1)S(1)} %all_to_all.52.x_ref, bf16[2,4,256,256]{3,2,1,0:T(8,128)(2,1)S(1)} %bitcast.60, bf16[3,4,256,256]{3,2,1,0:T(8,128)(2,1)S(1)} %bitcast.65, ...), custom_call_target="tpu_custom_call" | custom-call | tf_op jit(solution)/shard_map/lower0/pallas_call | solution.py:140
  97.6 18.2 %all_to_all.53.x_ref = bf16[8,4,16,256]{3,2,1,0:T(8,128)(2,1)S(1)} all-to-all(bf16[8,4,16,256]{3,2,1,0:T(8,128)(2,1)S(1)} %lower0.1), channel_id=1, replica_groups=mesh['row'=32,'col'=8] {'col'}, dimensions={0} | all-to-all | bytes 524288 | tf_op jit(solution)/shard_map/all_to_all | solution.py:279
  115.9 12.1 %all_to_all.54.refs_0_ = bf16[16,2,16,256]{3,2,1,0:T(8,128)(2,1)S(1)} all-to-all(bf16[16,2,16,256]{3,2,1,0:T(8,128)(2,1)S(1)} %get-tuple-element.19), channel_id=1, replica_groups={{0,8,16,24,32,40,48,56,64,72,80,88,96,104,112,120},{128,136,144,152,160..., dimensions={0} | all-to-all | bytes 524288 | tf_op jit(solution)/shard_map/all_to_all | solution.py:279
  128.0 4.2 %copy-done = bf16[80,256,256]{2,1,0:T(8,128)(2,1)S(1)} copy-done((bf16[80,256,256]{2,1,0:T(8,128)(2,1)S(1)}, bf16[80,256,256]{2,1,0:T(8,128)(2,1)}, u32[]{:S(2)}) %copy-start) | copy-done | bytes 10485784
  134.1 20.0 %all_to_all.55.refs_0_ = bf16[32,2,16,256]{3,2,1,0:T(8,128)(2,1)S(1)} all-to-all(bf16[32,2,16,256]{3,2,1,0:T(8,128)(2,1)S(1)} %get-tuple-element.20), channel_id=1, replica_groups=mesh['row'=32,'col'=8] {'row'}, dimensions={0} | all-to-all | bytes 1048576 | tf_op jit(solution)/shard_map/all_to_all | solution.py:279
  154.1 3.2 %lower2.1 = (bf16[16,1,16,256]{3,2,1,0:T(8,128)(2,1)S(1)}, f32[1,16,256]{2,1,0:T(8,128)}) custom-call(s32[13]{0:T(128)S(1)} %concatenate.6.s, bf16[32,2,16,256]{3,2,1,0:T(8,128)(2,1)S(1)} %all_to_all.55.refs_0_, bf16[8,10,256,256]{3,2,1,0:T(8,128)(2,1)S(1)} %bitcast.55, f32[1,16,256]{2,1,0:T(8,128)S(1)} %get-tuple-element.22.refs_2_), custom_call_target="tpu_custom_call" | custom-call | flops 536870912 | bytes 4194304 | tf_op jit(solution)/shard_map/lower2/pallas_call | solution.py:217
  157.3 12.9 %all_to_all.56.refs_0_ = bf16[16,1,16,256]{3,2,1,0:T(8,128)(2,1)S(1)} all-to-all(bf16[16,1,16,256]{3,2,1,0:T(8,128)(2,1)S(1)} %get-tuple-element.23), channel_id=1, replica_groups={{0,8,16,24,32,40,48,56,64,72,80,88,96,104,112,120},{128,136,144,152,160..., dimensions={0} | all-to-all | bytes 262144 | tf_op jit(solution)/shard_map/all_to_all | solution.py:279
  170.2 2.3 diagonal2.1
  172.5 14.8 %all_to_all.57.refs_2_ = bf16[32,1,16,256]{3,2,1,0:T(8,128)(2,1)S(1)} all-to-all(bf16[32,1,16,256]{3,2,1,0:T(8,128)(2,1)S(1)} %get-tuple-element.25), channel_id=1, replica_groups=mesh['row'=32,'col'=8] {'row'}, dimensions={0} | all-to-all | bytes 524288 | tf_op jit(solution)/shard_map/all_to_all | solution.py:279
  187.3 4.8 %copy-done.2 = bf16[96,256,256]{2,1,0:T(8,128)(2,1)S(1)} copy-done((bf16[96,256,256]{2,1,0:T(8,128)(2,1)S(1)}, bf16[96,256,256]{2,1,0:T(8,128)(2,1)}, u32[]{:S(2)}) %copy-start.2) | copy-done | bytes 12582936
  192.1 6.1 %lower3.1 = (bf16[32,1,16,256]{3,2,1,0:T(8,128)(2,1)}, f32[1,16,256]{2,1,0:T(8,128)}) custom-call(s32[13]{0:T(128)S(1)} %concatenate.6.s, bf16[32,2,16,256]{3,2,1,0:T(8,128)(2,1)S(1)} %all_to_all.55.refs_0_, bf16[8,12,256,256]{3,2,1,0:T(8,128)(2,1)S(1)} %bitcast.57, bf16[32,1,16,256]{3,2,1,0:T(8,128)(2,1)S(1)} %all_to_all.57.refs_2_, ...), custom_call_target="tpu_custom_call" | custom-call | flops 1610612736 | bytes 12582912 | tf_op jit(solution)/shard_map/lower3/pallas_call | solution.py:217
  198.2 3.9 %all-to-all-start.8 = ((bf16[32,1,16,256]{3,2,1,0:T(8,128)(2,1)}), bf16[32,1,16,256]{3,2,1,0:T(8,128)(2,1)S(1)}, u32[]{:S(2)}, u32[]{:S(2)}) async-start(bf16[32,1,16,256]{3,2,1,0:T(8,128)(2,1)} %get-tuple-element.27), calls=%async_computation.8 | async-start | bytes 524288 | tf_op jit(solution)/shard_map/all_to_all | solution.py:279
  202.2 10.4 %all-to-all-done.8.refs_0_ = bf16[32,1,16,256]{3,2,1,0:T(8,128)(2,1)S(1)} async-done(((bf16[32,1,16,256]{3,2,1,0:T(8,128)(2,1)}), bf16[32,1,16,256]{3,2,1,0:T(8,128)(2,1)S(1)}, u32[]{:S(2)}, u32[]{:S(2)}) %all-to-all-start.8) | async-done | bytes 262176 | tf_op jit(solution)/shard_map/all_to_all | solution.py:279
  214.8 3.3 %diagonal3.1 = (f32[8,1,16,256]{3,2,1,0:T(8,128)}, f32[1,16,256]{2,1,0:T(8,128)}) custom-call(s32[13]{0:T(128)S(1)} %concatenate.6.s, bf16[32,1,16,256]{3,2,1,0:T(8,128)(2,1)S(1)} %all-to-all-done.8.refs_0_, bf16[8,4,256,256]{3,2,1,0:T(8,128)(2,1)S(1)} %bitcast.63), custom_call_target="tpu_custom_call" | custom-call | flops 536870912 | bytes 4194304 | tf_op jit(solution)/shard_map/diagonal3/pallas_call | solution.py:217
  218.1 8.3 %all-to-all-start.9 = ((f32[8,1,16,256]{3,2,1,0:T(8,128)}), f32[8,1,16,256]{3,2,1,0:T(8,128)S(1)}, u32[]{:S(2)}, u32[]{:S(2)}) async-start(f32[8,1,16,256]{3,2,1,0:T(8,128)} %get-tuple-element.29), calls=%async_computation.9 | async-start | bytes 262144 | tf_op jit(solution)/shard_map/all_to_all | solution.py:279
  227.6 3.1 %assemble_early.1._ = f32[8,256,128]{2,1,0:T(8,128)} custom-call(f32[8,8,16,256]{3,2,1,0:T(8,128)S(1)} %bitcast.66), custom_call_target="tpu_custom_call" | custom-call | tf_op jit(solution)/shard_map/assemble_early/pallas_call | solution.py:243
  (65 shorter events, 22.7 us)
Async XLA Ops:
  6.5 121.5 %all-gather.9.cloned.1.call-start = ((), (), s32[]{:S(2)}) async-start(), calls=%async_computation.10 | async-start | bytes 11796480 | tf_op jit(solution)/shard_map/all_gather | solution.py:330
  9.6 2.1 copy-start.10
  11.8 1.4 copy-start.9
  13.2 1.6 copy-start.7
  14.5 172.8 %all-gather.11.cloned.1.call-start = ((), (), s32[]{:S(2)}) async-start(), calls=%async_computation.11 | async-start | bytes 14155776 | tf_op jit(solution)/shard_map/all_gather | solution.py:340
  14.8 19.9 %collective-permute-start = (bf16[4,256,128]{2,1,0:T(8,128)(2,1)S(1)}, bf16[4,256,128]{2,1,0:T(8,128)(2,1)S(1)}, u32[]{:S(2)}, u32[]{:S(2)}) collective-permute-start(bf16[4,256,128]{2,1,0:T(8,128)(2,1)S(1)} %fusion), channel_id=1, source_target_pairs={{0,48},{1,16},{2,40},{3,8},{4,32},{5,0},{6,56},{7,24},{8,25},{9,57... | collective-permute-start | bytes 786440 | tf_op jit(solution)/shard_map/ppermute | solution.py:61
  19.0 16.0 %collective-permute-start.1 = (bf16[4,256,128]{2,1,0:T(8,128)(2,1)S(1)}, bf16[4,256,128]{2,1,0:T(8,128)(2,1)S(1)}, u32[]{:S(2)}, u32[]{:S(2)}) collective-permute-start(bf16[4,256,128]{2,1,0:T(8,128)(2,1)S(1)} %fusion), channel_id=1, source_target_pairs={{0,112},{1,80},{2,104},{3,72},{4,96},{5,64},{6,120},{7,88},{8,89},... | collective-permute-start | bytes 786440 | tf_op jit(solution)/shard_map/ppermute | solution.py:61
  27.5 1.6 copy-start.8
  36.1 166.1 %all-gather.13.cloned.1.call-start = ((), (), s32[]{:S(2)}) async-start(), calls=%async_computation.12 | async-start | bytes 4718592 | tf_op jit(solution)/shard_map/all_gather | solution.py:340
  36.1 58.4 %copy-start.5 = (bf16[1,1,256,12,1,256]{5,2,4,3,1,0:T(8,128)(2,1)S(1)}, bf16[1,1,256,12,1,256]{5,2,4,3,1,0:T(8,128)(2,1)}, u32[]{:S(2)}) copy-start(bf16[1,1,256,12,1,256]{5,2,4,3,1,0:T(8,128)(2,1)} %param.12) | copy-start | bytes 4718596
  36.8 189.6 %all-gather.15.cloned.1.call-start = ((), (), s32[]{:S(2)}) async-start(), calls=%async_computation.13 | async-start | bytes 1179648 | tf_op jit(solution)/shard_map/all_gather | solution.py:363
  52.3 5.9 %collective-permute-start.2 = (bf16[4,16,256]{2,1,0:T(8,128)(2,1)S(1)}, bf16[4,16,256]{2,1,0:T(8,128)(2,1)S(1)}, u32[]{:S(2)}, u32[]{:S(2)}) collective-permute-start(bf16[4,16,256]{2,1,0:T(8,128)(2,1)S(1)} %convert_element_type.21), channel_id=1, source_target_pairs={{0,48},{1,16},{2,40},{3,8},{4,32},{5,0},{6,56},{7,24},{8,25},{9,57... | collective-permute-start | bytes 98312 | tf_op jit(solution)/shard_map/ppermute | solution.py:61
  58.2 36.4 %copy-start.3 = (bf16[1,1,256,28,1,256]{5,2,4,3,1,0:T(8,128)(2,1)S(1)}, bf16[1,1,256,28,1,256]{5,2,4,3,1,0:T(8,128)(2,1)}, u32[]{:S(2)}) copy-start(bf16[1,1,256,28,1,256]{5,2,4,3,1,0:T(8,128)(2,1)} %param.13) | copy-start | bytes 11010052
  128.0 4.2 %copy-start = (bf16[80,256,256]{2,1,0:T(8,128)(2,1)S(1)}, bf16[80,256,256]{2,1,0:T(8,128)(2,1)}, u32[]{:S(2)}) copy-start(bf16[80,256,256]{2,1,0:T(8,128)(2,1)} %all-gather.9.cloned.1.call-done) | copy-start | bytes 31457284
  132.2 21.8 %copy-start.1 = (bf16[80,256,256]{2,1,0:T(8,128)(2,1)S(1)}, bf16[80,256,256]{2,1,0:T(8,128)(2,1)}, u32[]{:S(2)}) copy-start(bf16[80,256,256]{2,1,0:T(8,128)(2,1)} %all-gather.9.cloned.1.call-done) | copy-start | bytes 31457284
  187.3 4.8 %copy-start.2 = (bf16[96,256,256]{2,1,0:T(8,128)(2,1)S(1)}, bf16[96,256,256]{2,1,0:T(8,128)(2,1)}, u32[]{:S(2)}) copy-start(bf16[96,256,256]{2,1,0:T(8,128)(2,1)} %all-gather.11.cloned.1.call-done) | copy-start | bytes 37748740
  198.2 14.3 %all-to-all-start.8 = ((bf16[32,1,16,256]{3,2,1,0:T(8,128)(2,1)}), bf16[32,1,16,256]{3,2,1,0:T(8,128)(2,1)S(1)}, u32[]{:S(2)}, u32[]{:S(2)}) async-start(bf16[32,1,16,256]{3,2,1,0:T(8,128)(2,1)} %get-tuple-element.27), calls=%async_computation.8 | async-start | bytes 524288 | tf_op jit(solution)/shard_map/all_to_all | solution.py:279
  212.6 2.2 copy-start.4
  218.1 13.6 %all-to-all-start.9 = ((f32[8,1,16,256]{3,2,1,0:T(8,128)}), f32[8,1,16,256]{3,2,1,0:T(8,128)S(1)}, u32[]{:S(2)}, u32[]{:S(2)}) async-start(f32[8,1,16,256]{3,2,1,0:T(8,128)} %get-tuple-element.29), calls=%async_computation.9 | async-start | bytes 262144 | tf_op jit(solution)/shard_map/all_to_all | solution.py:279
  226.4 1.2 copy-start.6
Sparse Core Ops, SparseCore 0:
  14.6 68.4 all-gather.8
  85.0 78.6 all-gather.10
  165.6 32.2 all-gather.12
  199.6 25.8 all-gather.14

commit v3 on v2

--- a/solution.py
+++ b/solution.py
@@ -322,10 +322,11 @@
     def masked(tiles, flags):
         return jnp.where(flags[:, None, None], tiles, jnp.zeros_like(tiles))
 
-    low = lax.optimization_barrier(jnp.swapaxes(inverse_low[:, 0, :, :, 0, :], 1, 2))
+    low = jnp.swapaxes(inverse_low[0:4, 0, :, :, 0, :], 1, 2)
+    upper_low = jnp.swapaxes(inverse_low[4:7, 0, :, :, 0, :], 1, 2)
     two = jnp.swapaxes(lower_two[0, 0, :, :, 0, :], 0, 1).reshape(3, 4, 256, 256)
     last = jnp.swapaxes(lower_top[0, 0, :, :, 0, :], 0, 1).reshape(7, 4, 256, 256)
-    low1, low2 = low[4:6].reshape(4, 256, 256), low[6]
+    low1, low2 = upper_low[0:2].reshape(4, 256, 256), upper_low[2]
     two1 = masked(two[2], listed(192 + row, 16 + 4 * h, 4))
     first = lax.all_gather(jnp.concatenate([low1, two1, low2]), "col")
     one = jnp.swapaxes(lower_one[:, 0, :, :, 0, :], 1, 2)
@@ -336,7 +337,7 @@
     second = masked(last[4:7].reshape(12, 256, 256), listed(224 + row, 16, 12))
     third = jnp.swapaxes(inverse_top[0, 0, :, :, 0, :], 0, 1)
 
-    part, second, third = diagonal0(place, near, far, low[0:4], (one, upper, keep), (second, third))
+    part, second, third = diagonal0(place, near, far, low, (one, upper, keep), (second, third))
     second, third = [lax.all_gather(value, "col") for value in (second, third)]
     sums = exchange(part, "col")
     solved0 = jnp.sum(sums.astype(F32), axis=0)

time: 240 us -> 237 us (0.988)
  local copies, waits for them, and re-layouts: 23.8 us -> 19.7 us
    unnamed x26 -> x27, local copies, waits for them, and re-layouts: 18.1 us -> 16 us
  transfers between devices with their start and end apart: 9 -> 9, of which waited for: 4 -> 4; matrix products, arithmetic and copies ran while one was open for 4% -> 3% of each run, Pallas kernels for 10% -> 10%
where the time goes in v3:
time: 237 us; the launch traced here: 236 us
  blocking collectives  129 us (54%)
  starting transfers between devices  27.4 us (12%)
  Pallas kernels  24.7 us (10%)
  local copies, waits for them, and re-layouts  19.7 us (8%)
  waiting for transfers between devices  15.2 us (6%)
  between operations  13.3 us (6%)
  other arithmetic  6.21 us (3%)
    all_to_all x8, blocking collectives, exchange(): lax.all_to_all(copies, axis, 0, 0, tiled=True, axis_index_groups=groups)  129 us
    pallas_call x5, Pallas kernels, multiply(): pl.pallas_call(kernel, out_shape=(jax.ShapeDtypeStruct((copies, n_out, 16...  16.7 us
    unnamed x27, local copies, waits for them, and re-layouts  16 us
    ppermute x3, starting transfers between devices, send(): return lax.ppermute(value, AXES, pairs)  15.1 us
    all_to_all x2, starting transfers between devices, exchange(): lax.all_to_all(copies, axis, 0, 0, tiled=True, axis_index_groups=groups)  12.2 us
    all_to_all x2, waiting for transfers between devices, exchange(): lax.all_to_all(copies, axis, 0, 0, tiled=True, axis_index_groups=groups)  11.4 us
  transfers between devices with their start and end apart: 9, of which 4 were waited for; matrix products, arithmetic and copies ran while one was open for 3% of the time, Pallas kernels for 10%

profile of v3, /device:TPU:1, one launch (start us, length us, event | category | flops | bytes accessed | tf_op | source)
XLA Modules:
  0.0 235.7 jit_solution(5639526650256785246)
XLA Ops:
  11.6 4.2 %collective-permute-start = (bf16[4,256,128]{2,1,0:T(8,128)(2,1)S(1)}, bf16[4,256,128]{2,1,0:T(8,128)(2,1)S(1)}, u32[]{:S(2)}, u32[]{:S(2)}) collective-permute-start(bf16[4,256,128]{2,1,0:T(8,128)(2,1)S(1)} %fusion), channel_id=1, source_target_pairs={{0,48},{1,16},{2,40},{3,8},{4,32},{5,0},{6,56},{7,24},{8,25},{9,57... | collective-permute-start | bytes 786440 | tf_op jit(solution)/shard_map/ppermute | solution.py:61
  15.8 5.6 %collective-permute-start.1 = (bf16[4,256,128]{2,1,0:T(8,128)(2,1)S(1)}, bf16[4,256,128]{2,1,0:T(8,128)(2,1)S(1)}, u32[]{:S(2)}, u32[]{:S(2)}) collective-permute-start(bf16[4,256,128]{2,1,0:T(8,128)(2,1)S(1)} %fusion), channel_id=1, source_target_pairs={{0,112},{1,80},{2,104},{3,72},{4,96},{5,64},{6,120},{7,88},{8,89},... | collective-permute-start | bytes 786440 | tf_op jit(solution)/shard_map/ppermute | solution.py:61
  26.9 2.9 %slice_select_fusion.refs_3_ = bf16[12,256,256]{2,1,0:T(8,128)(2,1)} fusion(bf16[28,256,256]{2,1,0:T(8,128)(2,1)} %bitcast.66, pred[12]{0:T(512)(128)(4,1)S(1)} %compare_reduce_fusion.1), kind=kLoop, calls=%fused_computation | loop fusion | flops 786432 | bytes 3145740 | tf_op jit(solution)/shard_map/jit(_where)/select_n | solution.py:323
  33.7 14.9 %all_to_all.50 = bf16[8,4,16,256]{3,2,1,0:T(8,128)(2,1)S(1)} all-to-all(bf16[8,4,16,256]{3,2,1,0:T(8,128)(2,1)S(1)} %get-tuple-element.18), channel_id=1, replica_groups=mesh['row'=32,'col'=8] {'col'}, dimensions={0} | all-to-all | bytes 524288 | tf_op jit(solution)/shard_map/all_to_all | solution.py:279
  48.7 5.3 %collective-permute-start.2 = (bf16[4,16,256]{2,1,0:T(8,128)(2,1)S(1)}, bf16[4,16,256]{2,1,0:T(8,128)(2,1)S(1)}, u32[]{:S(2)}, u32[]{:S(2)}) collective-permute-start(bf16[4,16,256]{2,1,0:T(8,128)(2,1)S(1)} %convert_element_type.21), channel_id=1, source_target_pairs={{0,48},{1,16},{2,40},{3,8},{4,32},{5,0},{6,56},{7,24},{8,25},{9,57... | collective-permute-start | bytes 98312 | tf_op jit(solution)/shard_map/ppermute | solution.py:61
  55.0 18.7 %all_to_all.51 = bf16[8,4,16,256]{3,2,1,0:T(8,128)(2,1)S(1)} all-to-all(bf16[8,4,16,256]{3,2,1,0:T(8,128)(2,1)S(1)} %broadcast_in_dim.41), channel_id=1, replica_groups={{0,32,64,96,128,160,192,224},{8,40,72,104,136,168,200,232},{16,48,80,11..., dimensions={0} | all-to-all | bytes 524288 | tf_op jit(solution)/shard_map/all_to_all | solution.py:279
  73.8 17.5 %all_to_all.52.x_ref = bf16[4,8,4,16,256]{4,3,2,1,0:T(8,128)(2,1)S(1)} all-to-all(bf16[4,8,4,16,256]{4,3,2,1,0:T(8,128)(2,1)S(1)} %broadcast_in_dim.42), channel_id=1, replica_groups={{0,8,16,24},{32,40,48,56},{64,72,80,88},{96,104,112,120},{128,136,144,1..., dimensions={0} | all-to-all | bytes 2097152 | tf_op jit(solution)/shard_map/all_to_all | solution.py:279
  91.3 3.1 %lower0.1 = bf16[8,4,16,256]{3,2,1,0:T(8,128)(2,1)S(1)} custom-call(s32[13]{0:T(128)S(1)} %concatenate.6.s, s32[128]{0:T(128)S(1)} %reshape.41.refs_2_.k, bf16[4,8,4,16,256]{4,3,2,1,0:T(8,128)(2,1)S(1)} %all_to_all.52.x_ref, bf16[2,4,256,256]{3,2,1,0:T(8,128)(2,1)S(1)} %bitcast.65, bf16[3,4,256,256]{3,2,1,0:T(8,128)(2,1)S(1)} %bitcast.71, ...), custom_call_target="tpu_custom_call" | custom-call | tf_op jit(solution)/shard_map/lower0/pallas_call | solution.py:140
  94.4 18.2 %all_to_all.53.x_ref = bf16[8,4,16,256]{3,2,1,0:T(8,128)(2,1)S(1)} all-to-all(bf16[8,4,16,256]{3,2,1,0:T(8,128)(2,1)S(1)} %lower0.1), channel_id=1, replica_groups=mesh['row'=32,'col'=8] {'col'}, dimensions={0} | all-to-all | bytes 524288 | tf_op jit(solution)/shard_map/all_to_all | solution.py:279
  112.7 12.1 %all_to_all.54.refs_0_ = bf16[16,2,16,256]{3,2,1,0:T(8,128)(2,1)S(1)} all-to-all(bf16[16,2,16,256]{3,2,1,0:T(8,128)(2,1)S(1)} %get-tuple-element.19), channel_id=1, replica_groups={{0,8,16,24,32,40,48,56,64,72,80,88,96,104,112,120},{128,136,144,152,160..., dimensions={0} | all-to-all | bytes 524288 | tf_op jit(solution)/shard_map/all_to_all | solution.py:279
  124.8 4.2 %copy-done = bf16[80,256,256]{2,1,0:T(8,128)(2,1)S(1)} copy-done((bf16[80,256,256]{2,1,0:T(8,128)(2,1)S(1)}, bf16[80,256,256]{2,1,0:T(8,128)(2,1)}, u32[]{:S(2)}) %copy-start) | copy-done | bytes 10485784
  130.9 20.0 %all_to_all.55.refs_0_ = bf16[32,2,16,256]{3,2,1,0:T(8,128)(2,1)S(1)} all-to-all(bf16[32,2,16,256]{3,2,1,0:T(8,128)(2,1)S(1)} %get-tuple-element.20), channel_id=1, replica_groups=mesh['row'=32,'col'=8] {'row'}, dimensions={0} | all-to-all | bytes 1048576 | tf_op jit(solution)/shard_map/all_to_all | solution.py:279
  150.9 3.2 %lower2.1 = (bf16[16,1,16,256]{3,2,1,0:T(8,128)(2,1)S(1)}, f32[1,16,256]{2,1,0:T(8,128)}) custom-call(s32[13]{0:T(128)S(1)} %concatenate.6.s, bf16[32,2,16,256]{3,2,1,0:T(8,128)(2,1)S(1)} %all_to_all.55.refs_0_, bf16[8,10,256,256]{3,2,1,0:T(8,128)(2,1)S(1)} %bitcast.60, f32[1,16,256]{2,1,0:T(8,128)S(1)} %get-tuple-element.22.refs_2_), custom_call_target="tpu_custom_call" | custom-call | flops 536870912 | bytes 4194304 | tf_op jit(solution)/shard_map/lower2/pallas_call | solution.py:217
  154.1 12.9 %all_to_all.56.refs_0_ = bf16[16,1,16,256]{3,2,1,0:T(8,128)(2,1)S(1)} all-to-all(bf16[16,1,16,256]{3,2,1,0:T(8,128)(2,1)S(1)} %get-tuple-element.23), channel_id=1, replica_groups={{0,8,16,24,32,40,48,56,64,72,80,88,96,104,112,120},{128,136,144,152,160..., dimensions={0} | all-to-all | bytes 262144 | tf_op jit(solution)/shard_map/all_to_all | solution.py:279
  167.0 2.3 diagonal2.1
  169.2 14.8 %all_to_all.57.refs_2_ = bf16[32,1,16,256]{3,2,1,0:T(8,128)(2,1)S(1)} all-to-all(bf16[32,1,16,256]{3,2,1,0:T(8,128)(2,1)S(1)} %get-tuple-element.25), channel_id=1, replica_groups=mesh['row'=32,'col'=8] {'row'}, dimensions={0} | all-to-all | bytes 524288 | tf_op jit(solution)/shard_map/all_to_all | solution.py:279
  184.1 4.8 %copy-done.2 = bf16[96,256,256]{2,1,0:T(8,128)(2,1)S(1)} copy-done((bf16[96,256,256]{2,1,0:T(8,128)(2,1)S(1)}, bf16[96,256,256]{2,1,0:T(8,128)(2,1)}, u32[]{:S(2)}) %copy-start.2) | copy-done | bytes 12582936
  188.9 6.1 %lower3.1 = (bf16[32,1,16,256]{3,2,1,0:T(8,128)(2,1)}, f32[1,16,256]{2,1,0:T(8,128)}) custom-call(s32[13]{0:T(128)S(1)} %concatenate.6.s, bf16[32,2,16,256]{3,2,1,0:T(8,128)(2,1)S(1)} %all_to_all.55.refs_0_, bf16[8,12,256,256]{3,2,1,0:T(8,128)(2,1)S(1)} %bitcast.62, bf16[32,1,16,256]{3,2,1,0:T(8,128)(2,1)S(1)} %all_to_all.57.refs_2_, ...), custom_call_target="tpu_custom_call" | custom-call | flops 1610612736 | bytes 12582912 | tf_op jit(solution)/shard_map/lower3/pallas_call | solution.py:217
  195.0 3.9 %all-to-all-start.8 = ((bf16[32,1,16,256]{3,2,1,0:T(8,128)(2,1)}), bf16[32,1,16,256]{3,2,1,0:T(8,128)(2,1)S(1)}, u32[]{:S(2)}, u32[]{:S(2)}) async-start(bf16[32,1,16,256]{3,2,1,0:T(8,128)(2,1)} %get-tuple-element.27), calls=%async_computation.8 | async-start | bytes 524288 | tf_op jit(solution)/shard_map/all_to_all | solution.py:279
  198.9 10.4 %all-to-all-done.8.refs_0_ = bf16[32,1,16,256]{3,2,1,0:T(8,128)(2,1)S(1)} async-done(((bf16[32,1,16,256]{3,2,1,0:T(8,128)(2,1)}), bf16[32,1,16,256]{3,2,1,0:T(8,128)(2,1)S(1)}, u32[]{:S(2)}, u32[]{:S(2)}) %all-to-all-start.8) | async-done | bytes 262176 | tf_op jit(solution)/shard_map/all_to_all | solution.py:279
  209.4 2.2 copy-done.4
  211.6 3.3 %diagonal3.1 = (f32[8,1,16,256]{3,2,1,0:T(8,128)}, f32[1,16,256]{2,1,0:T(8,128)}) custom-call(s32[13]{0:T(128)S(1)} %concatenate.6.s, bf16[32,1,16,256]{3,2,1,0:T(8,128)(2,1)S(1)} %all-to-all-done.8.refs_0_, bf16[8,4,256,256]{3,2,1,0:T(8,128)(2,1)S(1)} %bitcast.68), custom_call_target="tpu_custom_call" | custom-call | flops 536870912 | bytes 4194304 | tf_op jit(solution)/shard_map/diagonal3/pallas_call | solution.py:217
  214.8 8.3 %all-to-all-start.9 = ((f32[8,1,16,256]{3,2,1,0:T(8,128)}), f32[8,1,16,256]{3,2,1,0:T(8,128)S(1)}, u32[]{:S(2)}, u32[]{:S(2)}) async-start(f32[8,1,16,256]{3,2,1,0:T(8,128)} %get-tuple-element.29), calls=%async_computation.9 | async-start | bytes 262144 | tf_op jit(solution)/shard_map/all_to_all | solution.py:279
  224.4 3.1 %assemble_early.1._ = f32[8,256,128]{2,1,0:T(8,128)} custom-call(f32[8,8,16,256]{3,2,1,0:T(8,128)S(1)} %bitcast.72), custom_call_target="tpu_custom_call" | custom-call | tf_op jit(solution)/shard_map/assemble_early/pallas_call | solution.py:243
  (69 shorter events, 20.3 us)
Async XLA Ops:
  6.5 1.1 slice-start
  6.5 118.2 %all-gather.9.cloned.1.call-start = ((), (), s32[]{:S(2)}) async-start(), calls=%async_computation.10 | async-start | bytes 11796480 | tf_op jit(solution)/shard_map/all_gather | solution.py:331
  7.7 0.8 copy-start.10
  10.0 1.6 copy-start.8
  11.3 172.8 %all-gather.11.cloned.1.call-start = ((), (), s32[]{:S(2)}) async-start(), calls=%async_computation.11 | async-start | bytes 14155776 | tf_op jit(solution)/shard_map/all_gather | solution.py:341
  11.6 18.2 %collective-permute-start = (bf16[4,256,128]{2,1,0:T(8,128)(2,1)S(1)}, bf16[4,256,128]{2,1,0:T(8,128)(2,1)S(1)}, u32[]{:S(2)}, u32[]{:S(2)}) collective-permute-start(bf16[4,256,128]{2,1,0:T(8,128)(2,1)S(1)} %fusion), channel_id=1, source_target_pairs={{0,48},{1,16},{2,40},{3,8},{4,32},{5,0},{6,56},{7,24},{8,25},{9,57... | collective-permute-start | bytes 786440 | tf_op jit(solution)/shard_map/ppermute | solution.py:61
  15.8 16.0 %collective-permute-start.1 = (bf16[4,256,128]{2,1,0:T(8,128)(2,1)S(1)}, bf16[4,256,128]{2,1,0:T(8,128)(2,1)S(1)}, u32[]{:S(2)}, u32[]{:S(2)}) collective-permute-start(bf16[4,256,128]{2,1,0:T(8,128)(2,1)S(1)} %fusion), channel_id=1, source_target_pairs={{0,112},{1,80},{2,104},{3,72},{4,96},{5,64},{6,120},{7,88},{8,89},... | collective-permute-start | bytes 786440 | tf_op jit(solution)/shard_map/ppermute | solution.py:61
  21.4 1.2 copy-start.7
  22.7 1.2 slice-start.1
  23.9 1.0 copy-start.9
  32.9 166.0 %all-gather.13.cloned.1.call-start = ((), (), s32[]{:S(2)}) async-start(), calls=%async_computation.12 | async-start | bytes 4718592 | tf_op jit(solution)/shard_map/all_gather | solution.py:341
  32.9 58.4 %copy-start.5 = (bf16[1,1,256,12,1,256]{5,2,4,3,1,0:T(8,128)(2,1)S(1)}, bf16[1,1,256,12,1,256]{5,2,4,3,1,0:T(8,128)(2,1)}, u32[]{:S(2)}) copy-start(bf16[1,1,256,12,1,256]{5,2,4,3,1,0:T(8,128)(2,1)} %param.12) | copy-start | bytes 4718596
  33.6 189.5 %all-gather.15.cloned.1.call-start = ((), (), s32[]{:S(2)}) async-start(), calls=%async_computation.13 | async-start | bytes 1179648 | tf_op jit(solution)/shard_map/all_gather | solution.py:364
  48.7 6.3 %collective-permute-start.2 = (bf16[4,16,256]{2,1,0:T(8,128)(2,1)S(1)}, bf16[4,16,256]{2,1,0:T(8,128)(2,1)S(1)}, u32[]{:S(2)}, u32[]{:S(2)}) collective-permute-start(bf16[4,16,256]{2,1,0:T(8,128)(2,1)S(1)} %convert_element_type.21), channel_id=1, source_target_pairs={{0,48},{1,16},{2,40},{3,8},{4,32},{5,0},{6,56},{7,24},{8,25},{9,57... | collective-permute-start | bytes 98312 | tf_op jit(solution)/shard_map/ppermute | solution.py:61
  55.0 36.3 %copy-start.3 = (bf16[1,1,256,28,1,256]{5,2,4,3,1,0:T(8,128)(2,1)S(1)}, bf16[1,1,256,28,1,256]{5,2,4,3,1,0:T(8,128)(2,1)}, u32[]{:S(2)}) copy-start(bf16[1,1,256,28,1,256]{5,2,4,3,1,0:T(8,128)(2,1)} %param.13) | copy-start | bytes 11010052
  124.8 4.2 %copy-start = (bf16[80,256,256]{2,1,0:T(8,128)(2,1)S(1)}, bf16[80,256,256]{2,1,0:T(8,128)(2,1)}, u32[]{:S(2)}) copy-start(bf16[80,256,256]{2,1,0:T(8,128)(2,1)} %all-gather.9.cloned.1.call-done) | copy-start | bytes 31457284
  129.0 21.8 %copy-start.1 = (bf16[80,256,256]{2,1,0:T(8,128)(2,1)S(1)}, bf16[80,256,256]{2,1,0:T(8,128)(2,1)}, u32[]{:S(2)}) copy-start(bf16[80,256,256]{2,1,0:T(8,128)(2,1)} %all-gather.9.cloned.1.call-done) | copy-start | bytes 31457284
  184.1 4.8 %copy-start.2 = (bf16[96,256,256]{2,1,0:T(8,128)(2,1)S(1)}, bf16[96,256,256]{2,1,0:T(8,128)(2,1)}, u32[]{:S(2)}) copy-start(bf16[96,256,256]{2,1,0:T(8,128)(2,1)} %all-gather.11.cloned.1.call-done) | copy-start | bytes 37748740
  195.0 14.3 %all-to-all-start.8 = ((bf16[32,1,16,256]{3,2,1,0:T(8,128)(2,1)}), bf16[32,1,16,256]{3,2,1,0:T(8,128)(2,1)S(1)}, u32[]{:S(2)}, u32[]{:S(2)}) async-start(bf16[32,1,16,256]{3,2,1,0:T(8,128)(2,1)} %get-tuple-element.27), calls=%async_computation.8 | async-start | bytes 524288 | tf_op jit(solution)/shard_map/all_to_all | solution.py:279
  209.4 2.2 copy-start.4
  214.8 13.6 %all-to-all-start.9 = ((f32[8,1,16,256]{3,2,1,0:T(8,128)}), f32[8,1,16,256]{3,2,1,0:T(8,128)S(1)}, u32[]{:S(2)}, u32[]{:S(2)}) async-start(f32[8,1,16,256]{3,2,1,0:T(8,128)} %get-tuple-element.29), calls=%async_computation.9 | async-start | bytes 262144 | tf_op jit(solution)/shard_map/all_to_all | solution.py:279
  223.1 1.2 copy-start.6
Sparse Core Ops, SparseCore 0:
  11.4 68.4 all-gather.8
  81.8 78.6 all-gather.10
  162.4 32.2 all-gather.12
  196.4 25.8 all-gather.14

commit v4 on v3

--- a/solution.py
+++ b/solution.py
@@ -157,7 +157,7 @@
     )(place, keep, slices, one, two, last)
 
 
-def multiply(place, terms, base, n_out, copies, name, dtype=BF, early=None):
+def multiply(place, terms, base, n_out, copies, name, dtype=BF, early=None, halves=False, extra=None):
     steps = terms[0][3]
     early = early or ()
     lead = sum(value.shape[0] for value in early)
@@ -165,15 +165,18 @@
 
     def kernel(s, *refs):
         step = pl.program_id(0)
-        copy_ref, out_ref, acc = refs[-3:]
+        copy_ref, out_ref, acc = (*refs[-4:-2], refs[-1]) if halves else refs[-3:]
         h = s[3]
         tiles, blocks = [[] for _ in range(n_out)], [[] for _ in range(n_out)]
         for n, (_, _, _, _, _, picks) in enumerate(terms):
             x_ref, tile_ref = refs[2 * n : 2 * n + 2]
-            for t, c, a, o in picks(step, h):
+            for t, c, a, o, *other in picks(step, h):
                 for j in range(8):
                     tiles[o].append(tile_ref[j, t])
-                    blocks[o].append(x_ref[8 * c + j, a])
+                    block = x_ref[8 * c + j, a]
+                    if other:
+                        block = jnp.where(h == other[0], block, refs[2 * other[1]][8 * c + j, 1])
+                    blocks[o].append(block)
         for o in range(n_out):
             value = dot(jnp.concatenate(tiles[o], axis=1), jnp.concatenate(blocks[o], axis=1))
 
@@ -194,7 +197,14 @@
                 out_ref[lead + o] = value
                 cast = value.astype(dtype)
                 for r in range(copies):
-                    copy_ref[r, o] = cast
+                    if not halves:
+                        copy_ref[r, o] = cast
+                    elif r // 16 == o:
+                        copy_ref[r, 0] = cast
+                    else:
+                        refs[-2][r, 0] = cast
+            if extra is not None:
+                copy_ref[:, n_out : n_out + 1] = refs[-4][...]
             if early:
                 out_ref[0:4] = refs[2 * len(terms)][...]
                 out_ref[4:6] = refs[2 * len(terms) + 1][...]
@@ -214,20 +224,27 @@
     for value in early:
         args.append(value)
         specs.append(pl.BlockSpec(value.shape, lambda i, s: (0, 0, 0)))
+    if extra is not None:
+        args.append(extra)
+        specs.append(pl.BlockSpec(extra.shape, lambda i, s: (0, 0, 0, 0)))
+    wide = 1 if halves else n_out + (extra is not None)
+    apart = ((copies, 1, 16, 256),) if halves else ()
     return pl.pallas_call(
         kernel,
         out_shape=(
-            jax.ShapeDtypeStruct((copies, n_out, 16, 256), dtype),
+            jax.ShapeDtypeStruct((copies, wide, 16, 256), dtype),
             jax.ShapeDtypeStruct((total, 16, 256), F32),
-        ),
+        )
+        + tuple(jax.ShapeDtypeStruct(shape, BF) for shape in apart),
         grid_spec=pltpu.PrefetchScalarGridSpec(
             num_scalar_prefetch=1,
             grid=(steps,),
             in_specs=specs,
             out_specs=(
-                pl.BlockSpec((copies, n_out, 16, 256), lambda i, s: (0, 0, 0, 0)),
+                pl.BlockSpec((copies, wide, 16, 256), lambda i, s: (0, 0, 0, 0)),
                 pl.BlockSpec((total, 16, 256), lambda i, s: (0, 0, 0)),
-            ),
+            )
+            + tuple(pl.BlockSpec(shape, lambda i, s: (0, 0, 0, 0)) for shape in apart),
             scratch_shapes=[pltpu.VMEM((n_out, 256, 16), F32)],
         ),
         compiler_params=params(),
@@ -236,19 +253,23 @@
     )(place, *args)
 
 
-def assemble_early(slices):
-    def kernel(x_ref, out_ref):
-        out_ref[0] = x_ref[:, 0].reshape(128, 256).T
+def assemble_early(tiles):
+    def kernel(high_ref, fine_ref, out_ref):
+        value = high_ref[:, 0].astype(F32) + fine_ref[:, 0].astype(F32)
+        out_ref[0] = value.reshape(128, 256).T
 
     return pl.pallas_call(
         kernel,
         out_shape=jax.ShapeDtypeStruct((8, 256, 128), F32),
         grid=(7,),
-        in_specs=[pl.BlockSpec((8, 1, 16, 256), lambda i: (0, i, 0, 0))],
+        in_specs=[
+            pl.BlockSpec((8, 1, 16, 256), lambda i: (0, 4, i, 0)),
+            pl.BlockSpec((8, 1, 16, 256), lambda i: (0, 4, 8 + i, 0)),
+        ],
         out_specs=pl.BlockSpec((1, 256, 128), lambda i: (i, 0, 0)),
-        compiler_params=params(),
+        compiler_params=params(56),
         name="assemble_early",
-    )(slices)
+    )(tiles, tiles)
 
 
 def assemble_late(early, slices):
@@ -335,10 +356,10 @@
     keep = jnp.any(lists[None] == targets[:, None, None], axis=-1).astype(jnp.int32).reshape(128)
 
     second = masked(last[4:7].reshape(12, 256, 256), listed(224 + row, 16, 12))
-    third = jnp.swapaxes(inverse_top[0, 0, :, :, 0, :], 0, 1)
+    third = jnp.pad(jnp.swapaxes(inverse_top[0, 0, :, :, 0, :], 0, 1), ((0, 1), (0, 0), (0, 0)))
 
     part, second, third = diagonal0(place, near, far, low, (one, upper, keep), (second, third))
-    second, third = [lax.all_gather(value, "col") for value in (second, third)]
+    second = lax.all_gather(second, "col")
     sums = exchange(part, "col")
     solved0 = jnp.sum(sums.astype(F32), axis=0)
     slices = send(solved0.astype(BF), turn_pairs())
@@ -348,25 +369,28 @@
     copies, base2, base3 = finish0(sums, upper)
 
     reduced = exchange(copies, "row", HALVES)
-    copies, solved1 = multiply(
-        place, [(reduced, first, 0, 1, 4, lambda i, h: [(t, t % 2, t // 2, t // 2) for t in range(4)])], None, 2, 32, "diagonal1"
+    copies, solved1, other1 = multiply(
+        place, [(reduced, first, 0, 1, 4, lambda i, h: [(t, t % 2, t // 2, t // 2) for t in range(4)])], None, 2, 32, "diagonal1", halves=True
     )
     x1 = exchange(copies, "row")
 
     copies, _ = multiply(
-        place, [(x1, first, 4, 4, 1, lambda i, h: [(0, i, h, 0)])], base2, 1, 16, "lower2"
+        place, [(x1, first, 4, 4, 1, lambda i, h: [(0, i, 0, 0)])], base2, 1, 16, "lower2"
     )
     reduced = exchange(copies, "row", HALVES)
     copies, solved2 = multiply(
-        place, [(reduced, first, 8, 2, 1, lambda i, h: [(0, i, 0, 0)])], None, 1, 32, "diagonal2", early=(solved0, solved1)
+        place, [(reduced, first, 8, 2, 1, lambda i, h: [(0, i, 0, 0)])], None, 1, 32, "diagonal2", early=(solved0, solved1), extra=other1
     )
     x2 = exchange(copies, "row")
-    early = lax.all_gather(solved2, "col")
+    high = solved2.astype(BF)
+    fine = (solved2 - high.astype(F32)).astype(BF)
+    early = jnp.concatenate([high, fine]).reshape(1, 256, 256)
+    third = lax.all_gather(lax.dynamic_update_slice(third, early, (4, 0, 0)), "col")
 
     copies, _ = multiply(
         place,
         [
-            (x1, second, 0, 4, 2, lambda i, h: [(t, (2 * i + t) % 4, i // 2, 0) for t in range(2)]),
+            (x1, second, 0, 4, 2, lambda i, h: [(t, (2 * i + t) % 4, 0, 0, i // 2, 1) for t in range(2)]),
             (x2, second, 8, 4, 1, lambda i, h: [(0, i, 0, 0)]),
         ],
         base3, 1, 32, "lower3",
@@ -376,7 +400,7 @@
         place, [(reduced, third, 0, 4, 1, lambda i, h: [(0, i, 0, 0)])], None, 1, 8, "diagonal3", dtype=F32
     )
     late = exchange(copies, "col")
-    return assemble_late(assemble_early(early), late)[:, None]
+    return assemble_late(assemble_early(third), late)[:, None]
 
 
 def solution(mesh):

time: 237 us -> 237 us (level)
  blocking collectives: 129 us -> 143 us
  waiting for transfers between devices: 15.2 us -> 2.54 us
  starting transfers between devices: 27.4 us -> 23.1 us
    all_to_all x8 -> x9, blocking collectives: 129 us -> 143 us  [exchange(): lax.all_to_all(copies, axis, 0, 0, tiled=True, axis_index_groups=groups)]
    all_to_all x2 -> x1, waiting for transfers between devices: 11.4 us -> 0.38 us  [exchange(): lax.all_to_all(copies, axis, 0, 0, tiled=True, axis_index_groups=groups)]
    all_to_all x2 -> x1, starting transfers between devices: 12.2 us -> 8.01 us  [exchange(): lax.all_to_all(copies, axis, 0, 0, tiled=True, axis_index_groups=groups)]
    unnamed x27 -> x29, local copies, waits for them, and re-layouts: 16 us -> 16.4 us
  transfers between devices with their start and end apart: 9 -> 7, of which waited for: 4 -> 3; matrix products, arithmetic and copies ran while one was open for 3% -> 3% of each run, Pallas kernels for 10% -> 9%
where the time goes in v4:
time: 237 us; the launch traced here: 236 us
  blocking collectives  143 us (60%)
  Pallas kernels  25.8 us (11%)
  starting transfers between devices  23.1 us (10%)
  local copies, waits for them, and re-layouts  22 us (9%)
  between operations  13.4 us (6%)
  other arithmetic  6.25 us (3%)
  waiting for transfers between devices  2.54 us (1%)
    all_to_all x9, blocking collectives, exchange(): lax.all_to_all(copies, axis, 0, 0, tiled=True, axis_index_groups=groups)  143 us
    unnamed x29, local copies, waits for them, and re-layouts  16.4 us
    pallas_call x5, Pallas kernels, multiply(): pl.pallas_call(kernel, out_shape=(jax.ShapeDtypeStruct((copies, wide, 16,...  16 us
    ppermute x3, starting transfers between devices, send(): return lax.ppermute(value, AXES, pairs)  15 us
    all_to_all x1, starting transfers between devices, exchange(): lax.all_to_all(copies, axis, 0, 0, tiled=True, axis_index_groups=groups)  8.01 us
    pallas_call x1, Pallas kernels, assemble_early(): pl.pallas_call(kernel, out_shape=jax.ShapeDtypeStruct((8, 256, 128), F32)...  4.91 us
  transfers between devices with their start and end apart: 7, of which 3 were waited for; matrix products, arithmetic and copies ran while one was open for 3% of the time, Pallas kernels for 9%

profile of v4, /device:TPU:1, one launch (start us, length us, event | category | flops | bytes accessed | tf_op | source)
XLA Modules:
  0.0 236.1 jit_solution(8102362837793901206)
XLA Ops:
  12.3 4.1 %collective-permute-start = (bf16[4,256,128]{2,1,0:T(8,128)(2,1)}, bf16[4,256,128]{2,1,0:T(8,128)(2,1)S(1)}, u32[]{:S(2)}, u32[]{:S(2)}) collective-permute-start(bf16[4,256,128]{2,1,0:T(8,128)(2,1)} %fusion), channel_id=1, source_target_pairs={{0,48},{1,16},{2,40},{3,8},{4,32},{5,0},{6,56},{7,24},{8,25},{9,57... | collective-permute-start | bytes 786440 | tf_op jit(solution)/shard_map/ppermute | solution.py:61
  16.4 5.6 %collective-permute-start.1 = (bf16[4,256,128]{2,1,0:T(8,128)(2,1)}, bf16[4,256,128]{2,1,0:T(8,128)(2,1)S(1)}, u32[]{:S(2)}, u32[]{:S(2)}) collective-permute-start(bf16[4,256,128]{2,1,0:T(8,128)(2,1)} %fusion), channel_id=1, source_target_pairs={{0,112},{1,80},{2,104},{3,72},{4,96},{5,64},{6,120},{7,88},{8,89},... | collective-permute-start | bytes 786440 | tf_op jit(solution)/shard_map/ppermute | solution.py:61
  28.6 2.9 %slice_select_fusion.refs_3_ = bf16[12,256,256]{2,1,0:T(8,128)(2,1)} fusion(bf16[28,256,256]{2,1,0:T(8,128)(2,1)} %bitcast.66, pred[12]{0:T(512)(128)(4,1)S(1)} %compare_reduce_fusion.1), kind=kLoop, calls=%fused_computation | loop fusion | flops 786432 | bytes 3145740 | tf_op jit(solution)/shard_map/jit(_where)/select_n | solution.py:344
  34.5 15.3 %all_to_all.50 = bf16[8,4,16,256]{3,2,1,0:T(8,128)(2,1)S(1)} all-to-all(bf16[8,4,16,256]{3,2,1,0:T(8,128)(2,1)} %copy-done.7), channel_id=1, replica_groups=mesh['row'=32,'col'=8] {'col'}, dimensions={0} | all-to-all | bytes 524288 | tf_op jit(solution)/shard_map/all_to_all | solution.py:300
  49.8 5.3 %collective-permute-start.2 = (bf16[4,16,256]{2,1,0:T(8,128)(2,1)S(1)}, bf16[4,16,256]{2,1,0:T(8,128)(2,1)S(1)}, u32[]{:S(2)}, u32[]{:S(2)}) collective-permute-start(bf16[4,16,256]{2,1,0:T(8,128)(2,1)S(1)} %convert_element_type.32), channel_id=1, source_target_pairs={{0,48},{1,16},{2,40},{3,8},{4,32},{5,0},{6,56},{7,24},{8,25},{9,57... | collective-permute-start | bytes 98312 | tf_op jit(solution)/shard_map/ppermute | solution.py:61
  56.1 18.7 %all_to_all.51 = bf16[8,4,16,256]{3,2,1,0:T(8,128)(2,1)S(1)} all-to-all(bf16[8,4,16,256]{3,2,1,0:T(8,128)(2,1)S(1)} %broadcast_in_dim.41), channel_id=1, replica_groups={{0,32,64,96,128,160,192,224},{8,40,72,104,136,168,200,232},{16,48,80,11..., dimensions={0} | all-to-all | bytes 524288 | tf_op jit(solution)/shard_map/all_to_all | solution.py:300
  74.9 17.5 %all_to_all.52.x_ref = bf16[4,8,4,16,256]{4,3,2,1,0:T(8,128)(2,1)S(1)} all-to-all(bf16[4,8,4,16,256]{4,3,2,1,0:T(8,128)(2,1)S(1)} %broadcast_in_dim.42), channel_id=1, replica_groups={{0,8,16,24},{32,40,48,56},{64,72,80,88},{96,104,112,120},{128,136,144,1..., dimensions={0} | all-to-all | bytes 2097152 | tf_op jit(solution)/shard_map/all_to_all | solution.py:300
  92.4 3.1 %lower0.1 = bf16[8,4,16,256]{3,2,1,0:T(8,128)(2,1)S(1)} custom-call(s32[13]{0:T(128)S(1)} %concatenate.9.s, s32[128]{0:T(128)S(1)} %reshape.45.refs_2_.k, bf16[4,8,4,16,256]{4,3,2,1,0:T(8,128)(2,1)S(1)} %all_to_all.52.x_ref, bf16[2,4,256,256]{3,2,1,0:T(8,128)(2,1)S(1)} %bitcast.65, bf16[3,4,256,256]{3,2,1,0:T(8,128)(2,1)S(1)} %bitcast.71, ...), custom_call_target="tpu_custom_call" | custom-call | tf_op jit(solution)/shard_map/lower0/pallas_call | solution.py:140
  95.5 18.2 %all_to_all.53.x_ref = bf16[8,4,16,256]{3,2,1,0:T(8,128)(2,1)S(1)} all-to-all(bf16[8,4,16,256]{3,2,1,0:T(8,128)(2,1)S(1)} %lower0.1), channel_id=1, replica_groups=mesh['row'=32,'col'=8] {'col'}, dimensions={0} | all-to-all | bytes 524288 | tf_op jit(solution)/shard_map/all_to_all | solution.py:300
  113.8 12.1 %all_to_all.54.refs_0_ = bf16[16,2,16,256]{3,2,1,0:T(8,128)(2,1)S(1)} all-to-all(bf16[16,2,16,256]{3,2,1,0:T(8,128)(2,1)S(1)} %get-tuple-element.20), channel_id=1, replica_groups={{0,8,16,24,32,40,48,56,64,72,80,88,96,104,112,120},{128,136,144,152,160..., dimensions={0} | all-to-all | bytes 524288 | tf_op jit(solution)/shard_map/all_to_all | solution.py:300
  125.9 4.1 %copy-done = bf16[80,256,256]{2,1,0:T(8,128)(2,1)S(1)} copy-done((bf16[80,256,256]{2,1,0:T(8,128)(2,1)S(1)}, bf16[80,256,256]{2,1,0:T(8,128)(2,1)}, u32[]{:S(2)}) %copy-start) | copy-done | bytes 10485784
  130.0 1.9 diagonal1.1
  131.9 15.2 %all_to_all.55.refs_0_ = bf16[32,1,16,256]{3,2,1,0:T(8,128)(2,1)S(1)} all-to-all(bf16[32,1,16,256]{3,2,1,0:T(8,128)(2,1)S(1)} %get-tuple-element.21), channel_id=1, replica_groups=mesh['row'=32,'col'=8] {'row'}, dimensions={0} | all-to-all | bytes 524288 | tf_op jit(solution)/shard_map/all_to_all | solution.py:300
  147.1 3.2 %lower2.1 = (bf16[16,1,16,256]{3,2,1,0:T(8,128)(2,1)S(1)}, f32[1,16,256]{2,1,0:T(8,128)}) custom-call(s32[13]{0:T(128)S(1)} %concatenate.9.s, bf16[32,1,16,256]{3,2,1,0:T(8,128)(2,1)S(1)} %all_to_all.55.refs_0_, bf16[8,10,256,256]{3,2,1,0:T(8,128)(2,1)S(1)} %bitcast.60, f32[1,16,256]{2,1,0:T(8,128)S(1)} %get-tuple-element.23.refs_2_), custom_call_target="tpu_custom_call" | custom-call | flops 536870912 | bytes 4194304 | tf_op jit(solution)/shard_map/lower2/pallas_call | solution.py:232
  150.3 11.9 %all_to_all.56.refs_0_ = bf16[16,1,16,256]{3,2,1,0:T(8,128)(2,1)S(1)} all-to-all(bf16[16,1,16,256]{3,2,1,0:T(8,128)(2,1)S(1)} %get-tuple-element.24), channel_id=1, replica_groups={{0,8,16,24,32,40,48,56,64,72,80,88,96,104,112,120},{128,136,144,152,160..., dimensions={0} | all-to-all | bytes 262144 | tf_op jit(solution)/shard_map/all_to_all | solution.py:300
  162.2 1.7 diagonal2.1
  164.8 18.2 %all_to_all.57.refs_2_ = bf16[32,2,16,256]{3,2,1,0:T(8,128)(2,1)S(1)} all-to-all(bf16[32,2,16,256]{3,2,1,0:T(8,128)(2,1)S(1)} %get-tuple-element.27), channel_id=1, replica_groups=mesh['row'=32,'col'=8] {'row'}, dimensions={0} | all-to-all | bytes 1048576 | tf_op jit(solution)/shard_map/all_to_all | solution.py:300
  183.0 4.8 %copy-done.2 = bf16[96,256,256]{2,1,0:T(8,128)(2,1)S(1)} copy-done((bf16[96,256,256]{2,1,0:T(8,128)(2,1)S(1)}, bf16[96,256,256]{2,1,0:T(8,128)(2,1)}, u32[]{:S(2)}) %copy-start.2) | copy-done | bytes 12582936
  187.8 6.0 %lower3.1 = (bf16[32,1,16,256]{3,2,1,0:T(8,128)(2,1)S(1)}, f32[1,16,256]{2,1,0:T(8,128)}) custom-call(s32[13]{0:T(128)S(1)} %concatenate.9.s, bf16[32,1,16,256]{3,2,1,0:T(8,128)(2,1)S(1)} %all_to_all.55.refs_0_, bf16[8,12,256,256]{3,2,1,0:T(8,128)(2,1)S(1)} %bitcast.62, bf16[32,2,16,256]{3,2,1,0:T(8,128)(2,1)S(1)} %all_to_all.57.refs_2_, ...), custom_call_target="tpu_custom_call" | custom-call | flops 1610612736 | bytes 12582912 | tf_op jit(solution)/shard_map/lower3/pallas_call | solution.py:232
  193.8 16.0 %all_to_all.58.refs_0_ = bf16[32,1,16,256]{3,2,1,0:T(8,128)(2,1)S(1)} all-to-all(bf16[32,1,16,256]{3,2,1,0:T(8,128)(2,1)S(1)} %get-tuple-element.29), channel_id=1, replica_groups=mesh['row'=32,'col'=8] {'row'}, dimensions={0} | all-to-all | bytes 524288 | tf_op jit(solution)/shard_map/all_to_all | solution.py:300
  209.8 2.5 %copy-done.3 = bf16[8,5,256,256]{3,2,1,0:T(8,128)(2,1)S(1)} copy-done((bf16[8,5,256,256]{3,2,1,0:T(8,128)(2,1)S(1)}, bf16[8,5,256,256]{3,2,1,0:T(8,128)(2,1)}, u32[]{:S(2)}) %copy-start.3) | copy-done | bytes 5242904
  212.3 3.3 %diagonal3.1 = (f32[8,1,16,256]{3,2,1,0:T(8,128)}, f32[1,16,256]{2,1,0:T(8,128)}) custom-call(s32[13]{0:T(128)S(1)} %concatenate.9.s, bf16[32,1,16,256]{3,2,1,0:T(8,128)(2,1)S(1)} %all_to_all.58.refs_0_, bf16[8,5,256,256]{3,2,1,0:T(8,128)(2,1)S(1)} %copy-done.3), custom_call_target="tpu_custom_call" | custom-call | flops 536870912 | bytes 4194304 | tf_op jit(solution)/shard_map/diagonal3/pallas_call | solution.py:232
  215.6 8.0 %all-to-all-start.9 = ((f32[8,1,16,256]{3,2,1,0:T(8,128)}), f32[8,1,16,256]{3,2,1,0:T(8,128)S(1)}, u32[]{:S(2)}, u32[]{:S(2)}) async-start(f32[8,1,16,256]{3,2,1,0:T(8,128)} %get-tuple-element.32), calls=%async_computation.9 | async-start | bytes 262144 | tf_op jit(solution)/shard_map/all_to_all | solution.py:300
  223.6 4.9 %assemble_early.1._ = f32[8,256,128]{2,1,0:T(8,128)} custom-call(bf16[8,5,256,256]{3,2,1,0:T(8,128)(2,1)} %all-gather.6.cloned.1.call-done.refs_1_.high_ref.fine_ref, bf16[8,5,256,256]{3,2,1,0:T(8,128)(2,1)} %all-gather.6.cloned.1.call-done.refs_1_.high_ref.fine_ref), custom_call_target="tpu_custom_call" | custom-call | tf_op jit(solution)/shard_map/assemble_early/pallas_call | solution.py:261
  (71 shorter events, 18.4 us)
Async XLA Ops:
  6.5 1.1 slice-start
  6.5 119.4 %all-gather.8.cloned.1.call-start = ((), (), s32[]{:S(2)}) async-start(), calls=%async_computation.11 | async-start | bytes 11796480 | tf_op jit(solution)/shard_map/all_gather | solution.py:352
  7.7 0.8 copy-start.11
  10.0 1.6 copy-start.9
  11.3 171.7 %all-gather.10.cloned.1.call-start = ((), (), s32[]{:S(2)}) async-start(), calls=%async_computation.12 | async-start | bytes 14155776 | tf_op jit(solution)/shard_map/all_gather | solution.py:362
  12.3 19.3 %collective-permute-start = (bf16[4,256,128]{2,1,0:T(8,128)(2,1)}, bf16[4,256,128]{2,1,0:T(8,128)(2,1)S(1)}, u32[]{:S(2)}, u32[]{:S(2)}) collective-permute-start(bf16[4,256,128]{2,1,0:T(8,128)(2,1)} %fusion), channel_id=1, source_target_pairs={{0,48},{1,16},{2,40},{3,8},{4,32},{5,0},{6,56},{7,24},{8,25},{9,57... | collective-permute-start | bytes 786440 | tf_op jit(solution)/shard_map/ppermute | solution.py:61
  16.4 16.2 %collective-permute-start.1 = (bf16[4,256,128]{2,1,0:T(8,128)(2,1)}, bf16[4,256,128]{2,1,0:T(8,128)(2,1)S(1)}, u32[]{:S(2)}, u32[]{:S(2)}) collective-permute-start(bf16[4,256,128]{2,1,0:T(8,128)(2,1)} %fusion), channel_id=1, source_target_pairs={{0,112},{1,80},{2,104},{3,72},{4,96},{5,64},{6,120},{7,88},{8,89},... | collective-permute-start | bytes 786440 | tf_op jit(solution)/shard_map/ppermute | solution.py:61
  22.0 1.2 copy-start.8
  23.3 1.2 slice-start.1
  24.5 1.0 copy-start.10
  33.7 0.7 copy-start.7
  34.4 58.1 %copy-start.6 = (bf16[1,1,256,12,1,256]{5,2,4,3,1,0:T(8,128)(2,1)S(1)}, bf16[1,1,256,12,1,256]{5,2,4,3,1,0:T(8,128)(2,1)}, u32[]{:S(2)}) copy-start(bf16[1,1,256,12,1,256]{5,2,4,3,1,0:T(8,128)(2,1)} %param.12) | copy-start | bytes 4718596
  34.4 175.4 %all-gather.6.cloned.1.call-start = ((), (), s32[]{:S(2)}) async-start(), calls=%async_computation.10 | async-start | bytes 5898240 | tf_op jit(solution)/shard_map/all_gather | solution.py:388
  49.8 6.3 %collective-permute-start.2 = (bf16[4,16,256]{2,1,0:T(8,128)(2,1)S(1)}, bf16[4,16,256]{2,1,0:T(8,128)(2,1)S(1)}, u32[]{:S(2)}, u32[]{:S(2)}) collective-permute-start(bf16[4,16,256]{2,1,0:T(8,128)(2,1)S(1)} %convert_element_type.32), channel_id=1, source_target_pairs={{0,48},{1,16},{2,40},{3,8},{4,32},{5,0},{6,56},{7,24},{8,25},{9,57... | collective-permute-start | bytes 98312 | tf_op jit(solution)/shard_map/ppermute | solution.py:61
  56.1 36.3 %copy-start.4 = (bf16[1,1,256,28,1,256]{5,2,4,3,1,0:T(8,128)(2,1)S(1)}, bf16[1,1,256,28,1,256]{5,2,4,3,1,0:T(8,128)(2,1)}, u32[]{:S(2)}) copy-start(bf16[1,1,256,28,1,256]{5,2,4,3,1,0:T(8,128)(2,1)} %param.13) | copy-start | bytes 11010052
  125.9 4.1 %copy-start = (bf16[80,256,256]{2,1,0:T(8,128)(2,1)S(1)}, bf16[80,256,256]{2,1,0:T(8,128)(2,1)}, u32[]{:S(2)}) copy-start(bf16[80,256,256]{2,1,0:T(8,128)(2,1)} %all-gather.8.cloned.1.call-done) | copy-start | bytes 31457284
  130.0 17.1 %copy-start.1 = (bf16[80,256,256]{2,1,0:T(8,128)(2,1)S(1)}, bf16[80,256,256]{2,1,0:T(8,128)(2,1)}, u32[]{:S(2)}) copy-start(bf16[80,256,256]{2,1,0:T(8,128)(2,1)} %all-gather.8.cloned.1.call-done) | copy-start | bytes 31457284
  164.0 0.8 copy-start.5
  183.0 4.8 %copy-start.2 = (bf16[96,256,256]{2,1,0:T(8,128)(2,1)S(1)}, bf16[96,256,256]{2,1,0:T(8,128)(2,1)}, u32[]{:S(2)}) copy-start(bf16[96,256,256]{2,1,0:T(8,128)(2,1)} %all-gather.10.cloned.1.call-done) | copy-start | bytes 37748740
  209.8 2.5 %copy-start.3 = (bf16[8,5,256,256]{3,2,1,0:T(8,128)(2,1)S(1)}, bf16[8,5,256,256]{3,2,1,0:T(8,128)(2,1)}, u32[]{:S(2)}) copy-start(bf16[8,5,256,256]{3,2,1,0:T(8,128)(2,1)} %all-gather.6.cloned.1.call-done.refs_1_.high_ref.fine_ref) | copy-start | bytes 15728644
  215.6 13.3 %all-to-all-start.9 = ((f32[8,1,16,256]{3,2,1,0:T(8,128)}), f32[8,1,16,256]{3,2,1,0:T(8,128)S(1)}, u32[]{:S(2)}, u32[]{:S(2)}) async-start(f32[8,1,16,256]{3,2,1,0:T(8,128)} %get-tuple-element.32), calls=%async_computation.9 | async-start | bytes 262144 | tf_op jit(solution)/shard_map/all_to_all | solution.py:300
Sparse Core Ops, SparseCore 0:
  11.4 68.4 all-gather.7
  81.8 79.4 all-gather.9
  164.9 35.8 all-gather.5
